TPU v7x, 128 devices: a whole 4x4x4 slice. The times are simulated.
128 devices in a mesh: dp: 8 (over y, x_hi), ctx: 16 (over x_lo, z, core).
Axes of the slice: x: 4 (x_hi: 2, x_lo: 2; x = x_hi * 2 + x_lo), y: 4, z: 4, core: 2. Of those that a mesh axis runs over, the one named last changes fastest.
Arguments:
- signal: bfloat16 [8, 2048, 4096], P('dp', 'ctx'), may hold values from -6 to 6
- gate: bfloat16 [8, 2048, 4096], P('dp', 'ctx'), may hold values from -6 to 6
- cotangent: bfloat16 [8, 2048, 4096], P('dp', 'ctx'), may hold values from -6 to 6
- filter_taps: float32 [2048, 4096], P(None, 'ctx'), may hold values from -4 to 4
Outputs:
- signal_grad: bfloat16 [8, 2048, 4096], P('dp', 'ctx')
- gate_grad: bfloat16 [8, 2048, 4096], P('dp', 'ctx')
- taps_grad: float32 [2048, 4096], P('dp', 'ctx')
All inputs are finite; a program needn't handle non-finite values.
Results may differ from a plain program's by a relative error of at most 0.019.
Values may be sent and summed in bfloat16 or wider, within the bound.
No kernel may reach another device: no remote copies, remote signals or barrier semaphores. Data moves between devices by JAX's collectives and lax.ppermute only.
A program may use at most 128 MiB of HBM per device.

v0:
```python
import functools
import math

import jax
import jax.numpy as jnp
from jax import lax
from jax.sharding import PartitionSpec as P

close_einsum = functools.partial(
    jnp.einsum, precision=lax.Precision.HIGH, preferred_element_type=jnp.float32
)


def angle_table(first, second, modulus):
    index_prod = (
        jnp.arange(first, dtype=jnp.int32)[:, None]
        * jnp.arange(second, dtype=jnp.int32)[None, :]
        % modulus
    )
    phase = index_prod.astype(jnp.float32) * (-2.0 * math.pi / modulus)
    return (jnp.cos(phase), jnp.sin(phase))


def first_section(table, shaped):
    if shaped.dtype == jnp.bfloat16:
        table_high = table.astype(jnp.bfloat16)
        table_rest = (table - table_high.astype(jnp.float32)).astype(jnp.bfloat16)
        return jnp.einsum(
            "km,mpn->kpn", table_high, shaped, preferred_element_type=jnp.float32
        ) + jnp.einsum("km,mpn->kpn", table_rest, shaped, preferred_element_type=jnp.float32)
    return close_einsum("km,mpn->kpn", table, shaped)


def forward_transform(field, inner, outer):
    total = inner * outer
    half = inner // 2
    columns = field.shape[1]
    shaped = field.reshape(half, outer, columns)
    inner_cos, inner_sin = angle_table(inner, half, inner)
    section_real = first_section(inner_cos, shaped)
    section_imag = first_section(inner_sin, shaped)
    twist_cos, twist_sin = angle_table(inner, outer, total)
    twist_cos = twist_cos[:, :, None]
    twist_sin = twist_sin[:, :, None]
    turned_real = section_real * twist_cos - section_imag * twist_sin
    turned_imag = section_real * twist_sin + section_imag * twist_cos
    outer_cos, outer_sin = angle_table(outer, outer, outer)
    spec_real = close_einsum("lp,kpn->lkn", outer_cos, turned_real) - close_einsum(
        "lp,kpn->lkn", outer_sin, turned_imag
    )
    spec_imag = close_einsum("lp,kpn->lkn", outer_cos, turned_imag) + close_einsum(
        "lp,kpn->lkn", outer_sin, turned_real
    )
    return (spec_real.reshape(total, columns), spec_imag.reshape(total, columns))


def inverse_transform(spec_real, spec_imag, inner, outer):
    total = inner * outer
    half = inner // 2
    columns = spec_real.shape[1]
    shaped_real = spec_real.reshape(outer, inner, columns)
    shaped_imag = spec_imag.reshape(outer, inner, columns)
    outer_cos, outer_sin = angle_table(outer, outer, outer)
    section_real = close_einsum("pl,lkn->pkn", outer_cos, shaped_real) + close_einsum(
        "pl,lkn->pkn", outer_sin, shaped_imag
    )
    section_imag = close_einsum("pl,lkn->pkn", outer_cos, shaped_imag) - close_einsum(
        "pl,lkn->pkn", outer_sin, shaped_real
    )
    twist_cos, twist_sin = angle_table(outer, inner, total)
    twist_cos = twist_cos[:, :, None]
    twist_sin = twist_sin[:, :, None]
    turned_real = section_real * twist_cos + section_imag * twist_sin
    turned_imag = section_imag * twist_cos - section_real * twist_sin
    inner_cos, inner_sin = angle_table(half, inner, inner)
    result = close_einsum("qk,pkn->qpn", inner_cos, turned_real) + close_einsum(
        "qk,pkn->qpn", inner_sin, turned_imag
    )
    return result.reshape(half * outer, columns) * (1.0 / total)


def local(signal, gate, cotangent, filter_taps):
    ctx_count = lax.axis_size("ctx")
    tok_rows = signal.shape[1]
    width = signal.shape[2]
    per_device = width // ctx_count
    length = tok_rows * ctx_count
    total = 2 * length
    inner = math.gcd(total, 128)
    outer = total // inner
    scale = 1.0 / math.sqrt(length)
    taps_real, taps_imag = forward_transform(filter_taps * scale, inner, outer)
    local_signal = signal[0].reshape(tok_rows, ctx_count, per_device)
    local_cotangent = cotangent[0]
    local_gate = gate[0]
    moved_signal, moved_gate, moved_cotangent = (
        lax.all_to_all(local_signal, "ctx", split_axis=1, concat_axis=0, tiled=True),
        lax.all_to_all(
            local_gate.reshape(tok_rows, ctx_count, per_device),
            "ctx",
            split_axis=1,
            concat_axis=0,
            tiled=True,
        ),
        lax.all_to_all(
            local_cotangent.reshape(tok_rows, ctx_count, per_device),
            "ctx",
            split_axis=1,
            concat_axis=0,
            tiled=True,
        ),
    )
    chan_signal = moved_signal.reshape(length, per_device)
    chan_cotangent = moved_cotangent.reshape(length, per_device).astype(jnp.float32)
    chan_product = (
        chan_cotangent * moved_gate.reshape(length, per_device).astype(jnp.float32)
    ).astype(jnp.bfloat16)
    signal_real, signal_imag = forward_transform(chan_signal, inner, outer)
    product_real, product_imag = forward_transform(chan_product, inner, outer)
    conv = inverse_transform(
        taps_real * signal_real - taps_imag * signal_imag,
        taps_real * signal_imag + taps_imag * signal_real,
        inner,
        outer,
    ).astype(jnp.bfloat16)
    chan_signal_grad = inverse_transform(
        taps_real * product_real + taps_imag * product_imag,
        taps_real * product_imag - taps_imag * product_real,
        inner,
        outer,
    ).astype(jnp.bfloat16)
    taps_term = (
        inverse_transform(
            signal_real * product_real + signal_imag * product_imag,
            signal_real * product_imag - signal_imag * product_real,
            inner,
            outer,
        )
        * scale
    )
    second_field = (chan_cotangent * conv.astype(jnp.float32)).astype(jnp.bfloat16)
    back_signal, back_second = (
        lax.all_to_all(
            chan_signal_grad.reshape(length, 1, per_device),
            "ctx",
            split_axis=0,
            concat_axis=1,
            tiled=True,
        ),
        lax.all_to_all(
            second_field.reshape(length, 1, per_device),
            "ctx",
            split_axis=0,
            concat_axis=1,
            tiled=True,
        ),
    )
    signal_grad = back_signal.reshape(1, tok_rows, width)
    gate_grad = back_second.reshape(1, tok_rows, width)
    summed = lax.psum(taps_term.astype(jnp.bfloat16), "dp").astype(jnp.float32)
    share_rows = length // lax.axis_size("dp")
    taps_grad = lax.dynamic_slice_in_dim(summed, lax.axis_index("dp") * share_rows, share_rows, 0)
    return (signal_grad, gate_grad, taps_grad)


def solution(mesh):
    in_specs = (P("dp", "ctx", None), P("dp", "ctx", None), P("dp", "ctx", None), P(None, "ctx"))
    out_specs = (P("dp", "ctx", None), P("dp", "ctx", None), P("dp", "ctx"))
    return jax.shard_map(local, mesh=mesh, in_specs=in_specs, out_specs=out_specs, check_vma=False)
```

profile of v0, /device:TPU:0, one launch (start us, length us, event | category | flops | bytes accessed | tf_op | source)
XLA Modules:
  0.0 388.1 jit_solution(3582403948921642850)
XLA Ops:
  9.6 6.4 %all-to-all-start = ((bf16[128,16,256]{0,2,1:T(8,128)(2,1)}), bf16[128,16,256]{0,2,1:T(8,128)(2,1)S(1)}, u32[]{:S(2)}, u32[]{:S(2)}) async-start(bf16[128,16,256]{0,2,1:T(8,128)(2,1)} %bitcast.7), calls=%async_computation | async-start | bytes 2097152 | tf_op jit(solution)/shard_map/all_to_all | solution.py:105
  20.4 12.2 %all-to-all-done = bf16[128,16,256]{0,2,1:T(8,128)(2,1)S(1)} async-done(((bf16[128,16,256]{0,2,1:T(8,128)(2,1)}), bf16[128,16,256]{0,2,1:T(8,128)(2,1)S(1)}, u32[]{:S(2)}, u32[]{:S(2)}) %all-to-all-start) | async-done | bytes 1048608 | tf_op jit(solution)/shard_map/all_to_all | solution.py:105
  37.4 5.0 %fusion.56 = f32[128,32,256]{2,0,1:T(8,128)} fusion(f32[64,32,256]{2,1,0:T(8,128)S(1)} %bitcast.147), kind=kOutput, calls=%fused_computation.78 | convolution fusion | flops 402767872 | bytes 6291456 | tf_op jit(solution)/shard_map/km,mpn->kpn/dot_general | solution.py:31
  42.4 4.9 %fusion.58 = f32[128,32,256]{2,0,1:T(8,128)} fusion(f32[64,32,256]{2,1,0:T(8,128)S(1)} %bitcast.148), kind=kOutput, calls=%fused_computation.80 | convolution fusion | flops 402767872 | bytes 6291456 | tf_op jit(solution)/shard_map/km,mpn->kpn/dot_general | solution.py:31
  47.4 6.3 %all-to-all-done.1 = bf16[128,16,256]{0,2,1:T(8,128)(2,1)} async-done(((bf16[128,16,256]{0,2,1:T(8,128)(2,1)}), bf16[128,16,256]{0,2,1:T(8,128)(2,1)}, u32[]{:S(2)}, u32[]{:S(2)}) %all-to-all-start.1) | async-done | bytes 1048608 | tf_op jit(solution)/shard_map/all_to_all | solution.py:98
  53.6 4.9 %all-to-all-start.3 = ((bf16[128,16,256]{0,2,1:T(8,128)(2,1)}), bf16[128,16,256]{0,2,1:T(8,128)(2,1)}, u32[]{:S(2)}, u32[]{:S(2)}) async-start(bf16[128,16,256]{0,2,1:T(8,128)(2,1)} %bitcast.153), calls=%async_computation.3 | async-start | bytes 2097152 | tf_op jit(solution)/shard_map/all_to_all | solution.py:97
  66.5 8.6 %all-to-all-done.3 = bf16[128,16,256]{0,2,1:T(8,128)(2,1)} async-done(((bf16[128,16,256]{0,2,1:T(8,128)(2,1)}), bf16[128,16,256]{0,2,1:T(8,128)(2,1)}, u32[]{:S(2)}, u32[]{:S(2)}) %all-to-all-start.3) | async-done | bytes 1048608 | tf_op jit(solution)/shard_map/all_to_all | solution.py:97
  90.3 16.1 %multiply_subtract_fusion.4 = (f32[128,32,256]{2,0,1:T(8,128)}, f32[128,32,256]{2,0,1:T(8,128)}, f32[128,32,256]{2,0,1:T(8,128)}, f32[128,32,256]{2,0,1:T(8,128)...) fusion(f32[128,32,256]{2,0,1:T(8,128)} %convolution_add_fusion.4, f32[128,32]{0,1:T(8,128)S(1)} %get-tuple-element.39, ...), kind=kOutput, calls=%fused_computation.21 | convolution fusion | flops 154288128 | bytes 51412992 | tf_op jit(solution)/shard_map/km,mpn->kpn/dot_general | solution.py:30
  106.4 6.5 %fusion.30 = f32[32,128,256]{2,0,1:T(8,128)S(1)} fusion(f32[128,32,256]{2,0,1:T(8,128)} %get-tuple-element.37), kind=kOutput, calls=%fused_computation.48 | convolution fusion | flops 201340928 | bytes 8388608 | tf_op jit(solution)/shard_map/lp,kpn->lkn/dot_general | solution.py:48
  117.1 4.4 %fusion.20 = f32[32,128,256]{2,0,1:T(8,128)S(1)} fusion(f32[128,32,256]{2,0,1:T(8,128)S(1)} %copy-done.8), kind=kOutput, calls=%fused_computation.38 | convolution fusion | flops 201340928 | bytes 8388608 | tf_op jit(solution)/shard_map/lp,kpn->lkn/dot_general | solution.py:51
  129.9 6.7 %fusion.12 = f32[32,128,256]{2,0,1:T(8,128)} fusion(f32[128,32,256]{2,0,1:T(8,128)S(1)} %copy-done.7), kind=kOutput, calls=%fused_computation.30 | convolution fusion | flops 201340928 | bytes 8388608 | tf_op jit(solution)/shard_map/lp,kpn->lkn/dot_general | solution.py:51
  136.6 6.2 %fusion.36 = f32[32,128,256]{2,0,1:T(8,128)} fusion(f32[32,128,256]{2,0,1:T(8,128)S(1)} %fusion.30, f32[128,32,256]{2,0,1:T(8,128)S(1)} %copy-done.1), kind=kOutput, calls=%fused_computation.56 | convolution fusion | flops 202389504 | bytes 12582912 | tf_op jit(solution)/shard_map/lp,kpn->lkn/dot_general | solution.py:48
  142.8 6.1 %fusion.39 = f32[32,128,256]{2,0,1:T(8,128)} fusion(f32[32,128,256]{2,0,1:T(8,128)S(1)} %fusion.28, f32[128,32,256]{2,0,1:T(8,128)S(1)} %copy-done.1), kind=kOutput, calls=%fused_computation.57 | convolution fusion | flops 202389504 | bytes 12582912 | tf_op jit(solution)/shard_map/lp,kpn->lkn/dot_general | solution.py:51
  148.9 6.4 %fusion.45 = f32[32,128,256]{2,0,1:T(8,128)} fusion(f32[32,128,256]{2,0,1:T(8,128)S(1)} %fusion.20, f32[128,32,256]{2,0,1:T(8,128)S(1)} %copy-done), kind=kOutput, calls=%fused_computation.59 | convolution fusion | flops 202389504 | bytes 12582912 | tf_op jit(solution)/shard_map/lp,kpn->lkn/dot_general | solution.py:51
  155.4 6.1 %fusion.42 = f32[32,128,256]{2,0,1:T(8,128)} fusion(f32[32,128,256]{2,0,1:T(8,128)S(1)} %fusion.22, f32[128,32,256]{2,0,1:T(8,128)S(1)} %copy-done), kind=kOutput, calls=%fused_computation.58 | convolution fusion | flops 202389504 | bytes 12582912 | tf_op jit(solution)/shard_map/lp,kpn->lkn/dot_general | solution.py:48
  161.5 6.2 %fusion.48 = f32[32,128,256]{2,0,1:T(8,128)} fusion(f32[32,128,256]{2,0,1:T(8,128)S(1)} %fusion.14, f32[128,32,256]{2,0,1:T(8,128)S(1)} %copy-done.10), kind=kOutput, calls=%fused_computation.60 | convolution fusion | flops 202389504 | bytes 12582912 | tf_op jit(solution)/shard_map/lp,kpn->lkn/dot_general | solution.py:48
  167.7 20.4 %multiply_subtract_fusion.1 = (f32[32,128,256]{2,0,1:T(8,128)}, f32[32,128,256]{2,0,1:T(8,128)}, f32[32,128,256]{2,0,1:T(8,128)}, f32[32,128,256]{2,0,1:T(8,128)...) fusion(f32[32,128,256]{2,0,1:T(8,128)} %fusion.42, f32[32,128,256]{2,0,1:T(8,128)} %fusion.48, ...), kind=kOutput, calls=%fused_computation.14 | convolution fusion | flops 221263872 | bytes 54525952 | tf_op jit(solution)/shard_map/lp,kpn->lkn/dot_general | solution.py:51
  224.5 17.5 %multiply_add_fusion = (f32[32,128,256]{2,0,1:T(8,128)}, f32[32,128,256]{2,0,1:T(8,128)}, f32[32,128,256]{2,0,1:T(8,128)}, f32[32,128,256]{2,0,1:T(8,128)}, f32[32,128,256]{2,0,1:T(8,128)}, /*index=5*/f32[32,128,256]{2,0,1:T(8,128)}) fusion(f32[32,128,256]{2,0,1:T(8,128)} %convolution_add_fusion, f32[32,128]{0,1:T(8,128)S(1)} %get-tuple-element.41, ...), kind=kOutput, calls=%fused_computation.13 | convolution fusion | flops 221263872 | bytes 54558720 | tf_op jit(solution)/shard_map/pl,lkn->pkn/dot_general | solution.py:67
  242.0 5.8 %fusion = f32[64,32,256]{2,0,1:T(8,128)S(1)} fusion(f32[32,128,256]{2,0,1:T(8,128)} %get-tuple-element.16), kind=kOutput, calls=%fused_computation | convolution fusion | flops 402767872 | bytes 6291456 | tf_op jit(solution)/shard_map/qk,pkn->qpn/dot_general | solution.py:76
  273.3 5.8 %multiply_convert_fusion = bf16[64,32,256]{2,0,1:T(8,128)(2,1)S(1)} fusion(f32[64,32,256]{2,0,1:T(8,128)S(1)} %fusion, f32[32,128,256]{2,0,1:T(8,128)} %get-tuple-element.15), kind=kOutput, calls=%fused_computation.75 | convolution fusion | flops 404340736 | bytes 7340032 | tf_op jit(solution)/shard_map/qk,pkn->qpn/dot_general | solution.py:76
  280.7 5.9 %fusion.8 = f32[64,32,256]{2,0,1:T(8,128)S(1)} fusion(f32[32,128,256]{2,0,1:T(8,128)} %get-tuple-element.33), kind=kOutput, calls=%fused_computation.8 | convolution fusion | flops 402767872 | bytes 6291456 | tf_op jit(solution)/shard_map/qk,pkn->qpn/dot_general | solution.py:76
  293.7 5.7 %all-to-all-start.2 = ((bf16[16,2,16384]{2,1,0:T(2,128)(2,1)}), bf16[16,2,16384]{2,1,0:T(2,128)(2,1)}, u32[]{:S(2)}, u32[]{:S(2)}) async-start(bf16[16,2,16384]{2,1,0:T(2,128)(2,1)} %reshape.198), calls=%async_computation.2 | async-start | bytes 2097152 | tf_op jit(solution)/shard_map/all_to_all | solution.py:143
  302.6 23.6 %all-to-all-done.2 = bf16[16,2,16384]{2,1,0:T(2,128)(2,1)} async-done(((bf16[16,2,16384]{2,1,0:T(2,128)(2,1)}), bf16[16,2,16384]{2,1,0:T(2,128)(2,1)}, u32[]{:S(2)}, u32[]{:S(2)}) %all-to-all-start.2) | async-done | bytes 1048608 | tf_op jit(solution)/shard_map/all_to_all | solution.py:143
  332.7 46.7 %all-reduce.2.cloned.1.call-done = bf16[2048,256]{1,0:T(8,128)(2,1)} async-done(((bf16[2048,256]{1,0:T(8,128)(2,1)}), bf16[2048,256]{1,0:T(8,128)(2,1)}) %all-reduce.2.cloned.1.call-update) | async-done | bytes 1048592 | tf_op jit(solution)/shard_map/psum | solution.py:160
  (96 shorter events, 128.8 us)
Async XLA Ops:
  7.2 8.9 %copy-start.17 = (bf16[1,128,4096]{2,1,0:T(8,128)(2,1)S(1)}, bf16[1,128,4096]{2,1,0:T(8,128)(2,1)}, u32[]{:S(2)}) copy-start(bf16[1,128,4096]{2,1,0:T(8,128)(2,1)} %param.5) | copy-start | bytes 3145732
  7.2 10.2 %copy-start.18 = (bf16[1,128,4096]{2,1,0:T(8,128)(2,1)S(1)}, bf16[1,128,4096]{2,1,0:T(8,128)(2,1)}, u32[]{:S(2)}) copy-start(bf16[1,128,4096]{2,1,0:T(8,128)(2,1)} %param.4) | copy-start | bytes 3145732
  9.6 23.0 %all-to-all-start = ((bf16[128,16,256]{0,2,1:T(8,128)(2,1)}), bf16[128,16,256]{0,2,1:T(8,128)(2,1)S(1)}, u32[]{:S(2)}, u32[]{:S(2)}) async-start(bf16[128,16,256]{0,2,1:T(8,128)(2,1)} %bitcast.7), calls=%async_computation | async-start | bytes 2097152 | tf_op jit(solution)/shard_map/all_to_all | solution.py:105
  32.7 21.0 %all-to-all-start.1 = ((bf16[128,16,256]{0,2,1:T(8,128)(2,1)}), bf16[128,16,256]{0,2,1:T(8,128)(2,1)}, u32[]{:S(2)}, u32[]{:S(2)}) async-start(bf16[128,16,256]{0,2,1:T(8,128)(2,1)} %bitcast.154), calls=%async_computation.1 | async-start | bytes 2097152 | tf_op jit(solution)/shard_map/all_to_all | solution.py:98
  53.6 21.5 %all-to-all-start.3 = ((bf16[128,16,256]{0,2,1:T(8,128)(2,1)}), bf16[128,16,256]{0,2,1:T(8,128)(2,1)}, u32[]{:S(2)}, u32[]{:S(2)}) async-start(bf16[128,16,256]{0,2,1:T(8,128)(2,1)} %bitcast.153), calls=%async_computation.3 | async-start | bytes 2097152 | tf_op jit(solution)/shard_map/all_to_all | solution.py:97
  76.6 4.0 %copy-start.13 = (f32[128,32,256]{2,0,1:T(8,128)S(1)}, f32[128,32,256]{2,0,1:T(8,128)}, u32[]{:S(2)}) copy-start(f32[128,32,256]{2,0,1:T(8,128)} %fusion.77) | copy-start | bytes 12582916
  80.6 3.2 copy-start.12
  106.4 6.5 %copy-start.9 = (f32[128,32,256]{2,0,1:T(8,128)S(1)}, f32[128,32,256]{2,0,1:T(8,128)}, u32[]{:S(2)}) copy-start(f32[128,32,256]{2,0,1:T(8,128)} %get-tuple-element.37) | copy-start | bytes 12582916
  112.9 4.2 %copy-start.8 = (f32[128,32,256]{2,0,1:T(8,128)S(1)}, f32[128,32,256]{2,0,1:T(8,128)}, u32[]{:S(2)}) copy-start(f32[128,32,256]{2,0,1:T(8,128)} %get-tuple-element.35) | copy-start | bytes 12582916
  121.5 4.2 %copy-start.7 = (f32[128,32,256]{2,0,1:T(8,128)S(1)}, f32[128,32,256]{2,0,1:T(8,128)}, u32[]{:S(2)}) copy-start(f32[128,32,256]{2,0,1:T(8,128)} %get-tuple-element.22) | copy-start | bytes 12582916
  129.9 6.7 %copy-start.1 = (f32[128,32,256]{2,0,1:T(8,128)S(1)}, f32[128,32,256]{2,0,1:T(8,128)}, u32[]{:S(2)}) copy-start(f32[128,32,256]{2,0,1:T(8,128)} %get-tuple-element.38) | copy-start | bytes 12582916
  142.8 6.1 %copy-start = (f32[128,32,256]{2,0,1:T(8,128)S(1)}, f32[128,32,256]{2,0,1:T(8,128)}, u32[]{:S(2)}) copy-start(f32[128,32,256]{2,0,1:T(8,128)} %get-tuple-element.36) | copy-start | bytes 12582916
  155.4 6.2 %copy-start.10 = (f32[128,32,256]{2,0,1:T(8,128)S(1)}, f32[128,32,256]{2,0,1:T(8,128)}, u32[]{:S(2)}) copy-start(f32[128,32,256]{2,0,1:T(8,128)} %get-tuple-element.21) | copy-start | bytes 12582916
  188.1 4.3 %copy-start.6 = (f32[32,128,256]{2,0,1:T(8,128)S(1)}, f32[32,128,256]{2,0,1:T(8,128)}, u32[]{:S(2)}) copy-start(f32[32,128,256]{2,0,1:T(8,128)} %get-tuple-element.27) | copy-start | bytes 12582916
  194.3 3.9 %copy-start.5 = (f32[32,128,256]{2,0,1:T(8,128)S(1)}, f32[32,128,256]{2,0,1:T(8,128)}, u32[]{:S(2)}) copy-start(f32[32,128,256]{2,0,1:T(8,128)} %get-tuple-element.28) | copy-start | bytes 12582916
  198.3 3.9 %copy-start.3 = (f32[32,128,256]{2,0,1:T(8,128)S(1)}, f32[32,128,256]{2,0,1:T(8,128)}, u32[]{:S(2)}) copy-start(f32[32,128,256]{2,0,1:T(8,128)} %get-tuple-element.30) | copy-start | bytes 12582916
  210.4 4.0 %copy-start.11 = (f32[32,128,256]{2,0,1:T(8,128)S(1)}, f32[32,128,256]{2,0,1:T(8,128)}, u32[]{:S(2)}) copy-start(f32[32,128,256]{2,0,1:T(8,128)} %get-tuple-element.10) | copy-start | bytes 12582916
  214.4 2.2 copy-start.2
  242.0 5.9 %copy-start.16 = (f32[32,128,256]{2,0,1:T(8,128)S(1)}, f32[32,128,256]{2,0,1:T(8,128)}, u32[]{:S(2)}) copy-start(f32[32,128,256]{2,0,1:T(8,128)} %get-tuple-element.31) | copy-start | bytes 12582916
  247.9 3.6 copy-start.15
  269.6 24.1 %all-to-all-start.4 = ((bf16[16,2,16384]{2,1,0:T(2,128)(2,1)}), bf16[16,2,16384]{2,1,0:T(2,128)(2,1)S(1)}, u32[]{:S(2)}, u32[]{:S(2)}) async-start(bf16[16,2,16384]{2,1,0:T(2,128)(2,1)} %reshape.200), calls=%async_computation.4 | async-start | bytes 2097152 | tf_op jit(solution)/shard_map/all_to_all | solution.py:150
  273.2 106.2 %all-reduce.2.cloned.1.call-start = ((), (), s32[]{:S(2)}) async-start(), calls=%async_computation.5 | async-start | bytes 2097152 | tf_op jit(solution)/shard_map/psum | solution.py:160
  280.7 5.9 %copy-start.14 = (f32[32,128,256]{2,0,1:T(8,128)S(1)}, f32[32,128,256]{2,0,1:T(8,128)}, u32[]{:S(2)}) copy-start(f32[32,128,256]{2,0,1:T(8,128)} %get-tuple-element.34) | copy-start | bytes 12582916
  293.7 32.5 %all-to-all-start.2 = ((bf16[16,2,16384]{2,1,0:T(2,128)(2,1)}), bf16[16,2,16384]{2,1,0:T(2,128)(2,1)}, u32[]{:S(2)}, u32[]{:S(2)}) async-start(bf16[16,2,16384]{2,1,0:T(2,128)(2,1)} %reshape.198), calls=%async_computation.2 | async-start | bytes 2097152 | tf_op jit(solution)/shard_map/all_to_all | solution.py:143
  (1 other events, 2.2 us)
Sparse Core Ops, SparseCore 0:
  280.8 98.5 all-reduce.1
where the time goes:
time: 395 us; the launch traced here: 388 us
  matrix products  209 us (53%)
  waiting for transfers between devices  97.4 us (25%)
  local copies, waits for them, and re-layouts  28.7 us (7%)
  starting transfers between devices  25.1 us (6%)
  between operations  14.7 us (4%)
  other arithmetic  13.2 us (3%)
    psum x1, waiting for transfers between devices, local(): summed = lax.psum(taps_term.astype(jnp.bfloat16), 'dp').astype(jnp.float32)  46.7 us
    dot_general x3, matrix products, forward_transform(): close_einsum('lp,kpn->lkn', outer_sin, turned_real)  32.9 us
    dot_general x4, matrix products, first_section(): jnp.einsum('km,mpn->kpn', table_rest, shaped, preferred_element_type=jnp....  25.8 us
    dot_general x3, matrix products, inverse_transform(): close_einsum('pl,lkn->pkn', outer_sin, shaped_real)  25.3 us
    all_to_all x1, waiting for transfers between devices, local(): lax.all_to_all(chan_signal_grad.reshape(length, 1, per_device), 'ctx', sp...  23.6 us
    dot_general x3, matrix products, forward_transform(): close_einsum('lp,kpn->lkn', outer_cos, turned_real)  18.6 us
    unnamed x49, local copies, waits for them, and re-layouts  17.2 us
    dot_general x3, matrix products, inverse_transform(): close_einsum('qk,pkn->qpn', inner_sin, turned_imag)  15.3 us
  transfers between devices with their start and end apart: 6, of which 5 were waited for; matrix products, arithmetic and copies ran while one was open for 14% of the time, Pallas kernels for 0%

commit v1 on v0

v1 whole, which is shorter than its diff:
```python
import functools
import math

import jax
import jax.numpy as jnp
import ml_dtypes
import numpy as np
from jax import lax
from jax.experimental import pallas as pl
from jax.experimental.pallas import tpu as pltpu
from jax.sharding import PartitionSpec as P

F32 = jnp.float32
BF16 = jnp.bfloat16
RADIX = 16
INNER = 256
TOTAL = RADIX * INNER
BLOCKS = RADIX // 2
ROOT_HALF = math.sqrt(0.5)
COS_EIGHTH = math.cos(math.pi / 8)
SIN_EIGHTH = math.sin(math.pi / 8)
ROWS = 16
LANES = 128


def section_tables():
    column = np.arange(INNER)[None, :]
    forward = np.zeros((BLOCKS, 2 * INNER, 2 * INNER))
    half = INNER // 2
    row = np.arange(half)[:, None]
    for section in range(2):
        angle = 2 * np.pi * ((column * (RADIX * row + BLOCKS * section)) % TOTAL) / TOTAL
        place = slice(section * INNER, (section + 1) * INNER)
        forward[0, section * half : (section + 1) * half, place] = np.cos(angle)
        forward[0, INNER + section * half : INNER + (section + 1) * half, place] = -np.sin(angle)
    forward[0, INNER, :INNER] = np.cos(np.pi * column[0])
    row = np.arange(INNER)[:, None]
    for j in range(1, BLOCKS):
        angle = 2 * np.pi * ((column * (RADIX * row + j)) % TOTAL) / TOTAL
        forward[j] = np.block([[np.cos(angle), np.sin(angle)], [-np.sin(angle), np.cos(angle)]])
    weight = np.full((BLOCKS, 2 * INNER, 1), 2.0 / TOTAL)
    weight[0, 0] = weight[0, INNER] = 1.0 / TOTAL
    inverse = np.swapaxes(forward * weight, 1, 2)
    return (forward.astype(ml_dtypes.bfloat16), inverse.astype(ml_dtypes.bfloat16))


def half_sections(y0, y2, y4, y6):
    t, q = ROOT_HALF * (y2 - y6), ROOT_HALF * (y2 + y6)
    return (y0 + t, -(y4 + q)), (y0 - t, y4 - q)


def sections(x):
    x0, x1, x2, x3, x4, x5, x6, x7 = x
    a0, b0, a1, b1 = x0 + x4, x0 - x4, x1 + x5, x1 - x5
    a2, b2, a3, b3 = x2 + x6, x2 - x6, x3 + x7, x3 - x7
    even, odd = a0 + a2, a1 + a3
    t, q = ROOT_HALF * (b1 - b3), ROOT_HALF * (b1 + b3)
    (e1r, e1i), (e3r, e3i) = half_sections(x0, x2, x4, x6)
    (o1r, o1i), (o3r, o3i) = half_sections(x1, x3, x5, x7)
    m1r, m1i = COS_EIGHTH * o1r + SIN_EIGHTH * o1i, COS_EIGHTH * o1i - SIN_EIGHTH * o1r
    m3r, m3i = SIN_EIGHTH * o3r + COS_EIGHTH * o3i, SIN_EIGHTH * o3i - COS_EIGHTH * o3r
    return [
        (even + odd, even - odd),
        (e1r + m1r, e1i + m1i),
        (b0 + t, -(b2 + q)),
        (e3r + m3r, e3i + m3i),
        (a0 - a2, a3 - a1),
        (e3r - m3r, m3i - e3i),
        (b0 - t, b2 - q),
        (e1r - m1r, m1i - e1i),
    ]


def half_gather(e1r, e1i, e3r, e3i):
    t, w = ROOT_HALF * (e1r - e3r), ROOT_HALF * (e1i + e3i)
    return e1r + e3r, t - w, e3i - e1i, -(t + w)


def gather_sections(v):
    (p0, p8), (p1, q1), (p2, q2), (p3, q3), (p4, q4), (p5, q5), (p6, q6), (p7, q7) = v
    even, odd = p0 + p8, p0 - p8
    a0, a2, a1, a3 = even + p4, even - p4, odd - q4, odd + q4
    b0, b2 = p2 + p6, q6 - q2
    t, w = ROOT_HALF * (p2 - p6), ROOT_HALF * (q2 + q6)
    b1, b3 = t - w, -(t + w)
    e1r, e1i, m1r, m1i = p1 + p7, q1 - q7, p1 - p7, q1 + q7
    e3r, e3i, m3r, m3i = p3 + p5, q3 - q5, p3 - p5, q3 + q5
    o1r, o1i = COS_EIGHTH * m1r - SIN_EIGHTH * m1i, SIN_EIGHTH * m1r + COS_EIGHTH * m1i
    o3r, o3i = SIN_EIGHTH * m3r - COS_EIGHTH * m3i, COS_EIGHTH * m3r + SIN_EIGHTH * m3i
    y0, y2, y4, y6 = half_gather(e1r, e1i, e3r, e3i)
    y1, y3, y5, y7 = half_gather(o1r, o1i, o3r, o3i)
    return [
        a0 + b0 + y0,
        a1 + b1 + y1,
        a2 + b2 + y2,
        a3 + b3 + y3,
        a0 - b0 + y4,
        a1 - b1 + y5,
        a2 - b2 + y6,
        a3 - b3 + y7,
    ]


def product_kernel(signal_ref, gate_ref, cotangent_ref, out_ref):
    for piece in range(out_ref.shape[0]):
        lanes = pl.ds(piece * INNER, INNER)
        out_ref[piece, 0] = signal_ref[0, :, lanes]
        out_ref[piece, 1] = (
            cotangent_ref[0, :, lanes].astype(F32) * gate_ref[0, :, lanes].astype(F32)
        ).astype(BF16)


def send_fields(signal, gate, cotangent, count):
    rows, width = signal.shape[1:]
    steps = 4
    field = pl.BlockSpec((1, rows, width // steps), lambda i: (0, 0, i))
    return pl.pallas_call(
        product_kernel,
        grid=(steps,),
        in_specs=[field] * 3,
        out_specs=pl.BlockSpec((count // steps, 2, rows, width // count), lambda i: (i, 0, 0, 0)),
        out_shape=jax.ShapeDtypeStruct((count, 2, rows, width // count), BF16),
        name="product",
    )(signal, gate, cotangent)


def taps_kernel(scale, taps_ref, table_ref, out_ref, sections_ref):
    @pl.when(pl.program_id(0) == 0)
    def _():
        def rows_step(i, _):
            start = pl.multiple_of(i * ROWS, ROWS)
            for lane in range(INNER // LANES):
                lanes = pl.ds(lane * LANES, LANES)
                x = [taps_ref[pl.ds(n * INNER + start, ROWS), lanes] * scale for n in range(8)]
                for j, (real, imag) in enumerate(sections(x)):
                    sections_ref[j, pl.ds(start, ROWS), lanes] = real.astype(BF16)
                    sections_ref[j, pl.ds(INNER + start, ROWS), lanes] = imag.astype(BF16)
            return 0

        lax.fori_loop(0, INNER // ROWS, rows_step, 0)

    out_ref[0] = jnp.dot(table_ref[0], sections_ref[pl.program_id(0)], preferred_element_type=F32)


def taps_spectrum(taps, forward):
    length, width = taps.shape
    table = pl.BlockSpec((1, 2 * INNER, 2 * INNER), lambda j: (j, 0, 0))
    return pl.pallas_call(
        functools.partial(taps_kernel, 1.0 / math.sqrt(length)),
        grid=(BLOCKS,),
        in_specs=[pl.BlockSpec((length, width), lambda j: (0, 0)), table],
        out_specs=pl.BlockSpec((1, 2 * INNER, width), lambda j: (j, 0, 0)),
        out_shape=jax.ShapeDtypeStruct((BLOCKS, 2 * INNER, width), F32),
        scratch_shapes=[pltpu.VMEM((BLOCKS, 2 * INNER, width), BF16)],
        compiler_params=pltpu.CompilerParams(vmem_limit_bytes=32 << 20),
        name="taps_spectrum",
    )(taps, forward)


def multiply_spectra(out_ref, slot, left_ref, right_ref, conjugate):
    real, imag = pl.ds(0, INNER), pl.ds(INNER, INNER)
    lr, li, rr, ri = left_ref[real, :], left_ref[imag, :], right_ref[real, :], right_ref[imag, :]
    if conjugate:
        pr, pi = lr * rr + li * ri, lr * ri - li * rr
    else:
        pr, pi = lr * rr - li * ri, lr * ri + li * rr
    out_ref[slot, real, :] = pr.astype(BF16)
    out_ref[slot, imag, :] = pi.astype(BF16)

    @pl.when(pl.program_id(0) == 0)
    def _():
        top, low = pl.ds(0, ROWS), pl.ds(INNER, ROWS)
        first = lax.broadcasted_iota(jnp.int32, (ROWS, INNER), 0) == 0
        alone_r, alone_i = left_ref[top, :] * right_ref[top, :], left_ref[low, :] * right_ref[low, :]
        out_ref[slot, top, :] = jnp.where(first, alone_r, pr[:ROWS]).astype(BF16)
        out_ref[slot, low, :] = jnp.where(first, alone_i, pi[:ROWS]).astype(BF16)


def transforms_kernel(
    scale,
    fields_ref,
    taps_ref,
    forward_ref,
    inverse_ref,
    back_ref,
    term_ref,
    sections_ref,
    signal_ref,
    product_ref,
    spectra_ref,
    parts_ref,
):
    step = pl.program_id(0)

    @pl.when(step == 0)
    def _():
        def rows_step(i, _):
            start = pl.multiple_of((i % 8) * ROWS, ROWS)
            place = pl.multiple_of(i * ROWS, ROWS)
            for field in range(2):
                for lane in range(INNER // LANES):
                    lanes = pl.ds(lane * LANES, LANES)
                    x = [
                        fields_ref[2 * n + i // 8, field, pl.ds(start, ROWS), lanes].astype(F32)
                        for n in range(8)
                    ]
                    for j, (real, imag) in enumerate(sections(x)):
                        sections_ref[field, j, pl.ds(place, ROWS), lanes] = real.astype(BF16)
                        sections_ref[field, j, pl.ds(INNER + place, ROWS), lanes] = imag.astype(BF16)
            return 0

        lax.fori_loop(0, INNER // ROWS, rows_step, 0)

    table, back_table = forward_ref[0], inverse_ref[0]
    signal_ref[...] = jnp.dot(table, sections_ref[0, step], preferred_element_type=F32)
    product_ref[...] = jnp.dot(table, sections_ref[1, step], preferred_element_type=F32)
    multiply_spectra(spectra_ref, 0, taps_ref.at[0], product_ref, True)
    multiply_spectra(spectra_ref, 1, taps_ref.at[0], signal_ref, False)
    multiply_spectra(spectra_ref, 2, signal_ref, product_ref, True)
    for out in range(3):
        parts_ref[out, step] = jnp.dot(back_table, spectra_ref[out], preferred_element_type=F32)

    @pl.when(step == BLOCKS - 1)
    def _():
        def rows_step(i, _):
            start = pl.multiple_of((i % 8) * ROWS, ROWS)
            place = pl.multiple_of(i * ROWS, ROWS)
            for out in range(3):
                for lane in range(INNER // LANES):
                    lanes = pl.ds(lane * LANES, LANES)
                    v = [
                        (
                            parts_ref[out, j, pl.ds(place, ROWS), lanes],
                            parts_ref[out, j, pl.ds(INNER + place, ROWS), lanes],
                        )
                        for j in range(BLOCKS)
                    ]
                    for n, y in enumerate(gather_sections(v)):
                        if out < 2:
                            back_ref[2 * n + i // 8, out, pl.ds(start, ROWS), lanes] = y.astype(BF16)
                        else:
                            term_ref[pl.ds(n * INNER + place, ROWS), lanes] = (y * scale).astype(BF16)
            return 0

        lax.fori_loop(0, INNER // ROWS, rows_step, 0)


def transforms(fields, taps_spec, forward, inverse):
    count, _, rows, width = fields.shape
    length = count * rows
    table = pl.BlockSpec((1, 2 * INNER, 2 * INNER), lambda j: (j, 0, 0))
    whole = pl.BlockSpec((count, 2, rows, width), lambda j: (0, 0, 0, 0))
    block = (2 * INNER, width)
    return pl.pallas_call(
        functools.partial(transforms_kernel, 1.0 / math.sqrt(length)),
        grid=(BLOCKS,),
        in_specs=[whole, pl.BlockSpec((1,) + block, lambda j: (j, 0, 0)), table, table],
        out_specs=[whole, pl.BlockSpec((length, width), lambda j: (0, 0))],
        out_shape=[
            jax.ShapeDtypeStruct(fields.shape, BF16),
            jax.ShapeDtypeStruct((length, width), BF16),
        ],
        scratch_shapes=[
            pltpu.VMEM((2, BLOCKS) + block, BF16),
            pltpu.VMEM(block, F32),
            pltpu.VMEM(block, F32),
            pltpu.VMEM((3,) + block, BF16),
            pltpu.VMEM((3, BLOCKS) + block, F32),
        ],
        compiler_params=pltpu.CompilerParams(vmem_limit_bytes=48 << 20),
        name="transforms",
    )(fields, taps_spec, forward, inverse)


def outputs_kernel(back_ref, cotangent_ref, signal_grad_ref, gate_grad_ref):
    for piece in range(back_ref.shape[0]):
        lanes = pl.ds(piece * INNER, INNER)
        signal_grad_ref[0, :, lanes] = back_ref[piece, 0]
        gate_grad_ref[0, :, lanes] = (
            cotangent_ref[0, :, lanes].astype(F32) * back_ref[piece, 1].astype(F32)
        ).astype(BF16)


def place_outputs(back, cotangent):
    count, _, rows, width = back.shape
    steps = 4
    field = pl.BlockSpec((1, rows, cotangent.shape[2] // steps), lambda i: (0, 0, i))
    return pl.pallas_call(
        outputs_kernel,
        grid=(steps,),
        in_specs=[
            pl.BlockSpec((count // steps, 2, rows, width), lambda i: (i, 0, 0, 0)),
            field,
        ],
        out_specs=[field, field],
        out_shape=[jax.ShapeDtypeStruct(cotangent.shape, BF16)] * 2,
        name="outputs",
    )(back, cotangent)


def exchange(term, mine, pairs):
    keep = lax.dynamic_index_in_dim(term, mine, 0, keepdims=False)
    away = lax.dynamic_index_in_dim(term, 1 - mine, 0, keepdims=False).astype(BF16)
    return keep.astype(F32) + lax.ppermute(away, "dp", pairs).astype(F32)


def sum_over_sequences(term):
    devices = lax.axis_size("dp")
    index = lax.axis_index("dp")
    width = term.shape[1]
    share = term.shape[0] // devices
    y_pairs = [(d, ((3 - d // 2) * 2) + d % 2) for d in range(devices)]
    total = exchange(term.reshape(2, devices // 2, share, width), index // 4, y_pairs)
    total = exchange(total.reshape(2, devices // 4, share, width), (index // 2) % 2, [(d, d ^ 2) for d in range(devices)])
    return exchange(total.reshape(2, share, width), index % 2, [(d, d ^ 1) for d in range(devices)])


def local(signal, gate, cotangent, filter_taps):
    count = lax.axis_size("ctx")
    forward, inverse = section_tables()
    fields = lax.all_to_all(send_fields(signal, gate, cotangent, count), "ctx", 0, 0, tiled=True)
    taps_spec = taps_spectrum(filter_taps, forward)
    back, term = transforms(fields, taps_spec, forward, inverse)
    back = lax.all_to_all(back, "ctx", 0, 0, tiled=True)
    taps_grad = sum_over_sequences(term)
    signal_grad, gate_grad = place_outputs(back, cotangent)
    return (signal_grad, gate_grad, taps_grad)


def solution(mesh):
    in_specs = (P("dp", "ctx", None), P("dp", "ctx", None), P("dp", "ctx", None), P(None, "ctx"))
    out_specs = (P("dp", "ctx", None), P("dp", "ctx", None), P("dp", "ctx"))
    return jax.shard_map(local, mesh=mesh, in_specs=in_specs, out_specs=out_specs, check_vma=False)
```

time: 395 us -> 105 us (0.27); the launches traced: 388 us -> 104 us
  matrix products: 209 us -> 0 us
  waiting for transfers between devices: 97.4 us -> 43.7 us
  Pallas kernels: 0 us -> 28.4 us
  local copies, waits for them, and re-layouts: 28.7 us -> 10.2 us
  between operations: 14.7 us -> 0.74 us
  other arithmetic: 13.2 us -> 2.97 us
  starting transfers between devices: 25.1 us -> 18.2 us
    dot_general x40 -> x0, matrix products: 209 us -> none  [the longest x3 32.9 us: forward_transform(): close_einsum('lp,kpn->lkn', outer_sin, turned_real)]
    psum x1 -> x0, waiting for transfers between devices: 46.7 us -> none  [local(): summed = lax.psum(taps_term.astype(jnp.bfloat16), 'dp').astype(jnp.float32)]
    all_to_all x5 -> x2, waiting for transfers between devices: 50.6 us -> 19.6 us  [the longest x1 19.6 us: local(): lax.all_to_all(send_fields(signal, gate, cotangent, count), 'ctx', 0, 0,...]
    pallas_call x0 -> x4, Pallas kernels: none -> 28.4 us  [the longest x1 16.9 us: transforms(): pl.pallas_call(functools.partial(transforms_kernel, 1.0 / math.sqrt(lengt...]
    ppermute x0 -> x3, waiting for transfers between devices: none -> 24.1 us  [exchange(): return keep.astype(F32) + lax.ppermute(away, 'dp', pairs).astype(F32)]
    all_to_all x5 -> x2, starting transfers between devices: 25 us -> 11.9 us  [the longest x1 6.43 us: local(): lax.all_to_all(send_fields(signal, gate, cotangent, count), 'ctx', 0, 0,...]
    convert_element_type x6 -> x0, other arithmetic: 11 us -> none  [the longest x2 4.53 us: local(): (chan_cotangent * conv.astype(jnp.float32)).astype(jnp.bfloat16)]
    convert_element_type x6 -> x2, local copies, waits for them, and re-layouts: 8.74 us -> 0.05 us  [exchange(): lax.dynamic_index_in_dim(term, 1 - mine, 0, keepdims=False).astype(BF16)]
  transfers between devices with their start and end apart: 6 -> 5, of which waited for: 5 -> 4; matrix products, arithmetic and copies ran while one was open for 14% -> 4% of each run, Pallas kernels for 0% -> 3%
where the time goes in v1:
time: 105 us; the launch traced here: 104 us
  waiting for transfers between devices  43.7 us (42%)
  Pallas kernels  28.4 us (27%)
  starting transfers between devices  18.2 us (17%)
  local copies, waits for them, and re-layouts  10.2 us (10%)
  other arithmetic  2.97 us (3%)
    ppermute x3, waiting for transfers between devices, exchange(): return keep.astype(F32) + lax.ppermute(away, 'dp', pairs).astype(F32)  24.1 us
    all_to_all x1, waiting for transfers between devices, local(): lax.all_to_all(send_fields(signal, gate, cotangent, count), 'ctx', 0, 0,...  19.6 us
    pallas_call x1, Pallas kernels, transforms(): pl.pallas_call(functools.partial(transforms_kernel, 1.0 / math.sqrt(lengt...  16.9 us
    unnamed x12, local copies, waits for them, and re-layouts  9.35 us
    all_to_all x1, starting transfers between devices, local(): lax.all_to_all(send_fields(signal, gate, cotangent, count), 'ctx', 0, 0,...  6.43 us
    ppermute x3, starting transfers between devices, exchange(): return keep.astype(F32) + lax.ppermute(away, 'dp', pairs).astype(F32)  6.24 us
    all_to_all x1, starting transfers between devices, local(): back = lax.all_to_all(back, 'ctx', 0, 0, tiled=True)  5.51 us
    pallas_call x1, Pallas kernels, send_fields(): pl.pallas_call(product_kernel, grid=(steps,), in_specs=[field] * 3, out_s...  4.05 us
  transfers between devices with their start and end apart: 5, of which 4 were waited for; matrix products, arithmetic and copies ran while one was open for 4% of the time, Pallas kernels for 3%

profile of v1, /device:TPU:0, one launch (start us, length us, event | category | flops | bytes accessed | tf_op | source)
XLA Modules:
  0.0 104.1 jit_solution(7624694749991271486)
XLA Ops:
  0.6 4.0 %product.1 = bf16[16,2,128,256]{3,2,1,0:T(8,128)(2,1)} custom-call(bf16[1,128,4096]{2,1,0:T(8,128)(2,1)} %signal_ref.1, bf16[1,128,4096]{2,1,0:T(8,128)(2,1)} %gate_ref.1, bf16[1,128,4096]{2,1,0:T(8,128)(2,1)} %cotangent_ref.3), custom_call_target="tpu_custom_call" | custom-call | tf_op jit(solution)/shard_map/product/pallas_call | solution.py:117
  4.7 6.4 %all-to-all-start = ((bf16[16,2,128,256]{3,2,1,0:T(8,128)(2,1)}), bf16[16,2,128,256]{3,2,1,0:T(8,128)(2,1)S(1)}, u32[]{:S(2)}, u32[]{:S(2)}) async-start(bf16[16,2,128,256]{3,2,1,0:T(8,128)(2,1)} %product.1), calls=%async_computation | async-start | bytes 4194304 | tf_op jit(solution)/shard_map/all_to_all | solution.py:321
  11.1 0.0 copy-start
  11.1 2.2 %copy-done = bf16[8,512,512]{2,1,0:T(8,128)(2,1)S(1)} copy-done((bf16[8,512,512]{2,1,0:T(8,128)(2,1)S(1)}, bf16[8,512,512]{2,1,0:T(8,128)(2,1)}, u32[]{:S(2)}) %copy-start) | copy-done | bytes 4194328
  13.3 1.6 %copy-done.2 = f32[2048,256]{1,0:T(8,128)S(1)} copy-done((f32[2048,256]{1,0:T(8,128)S(1)}, f32[2048,256]{1,0:T(8,128)}, u32[]{:S(2)}) %copy-start.2) | copy-done | bytes 2097176
  14.9 3.4 %taps_spectrum.1.taps_ref = f32[8,512,256]{2,1,0:T(8,128)S(1)} custom-call(f32[2048,256]{1,0:T(8,128)S(1)} %copy-done.2, bf16[8,512,512]{2,1,0:T(8,128)(2,1)S(1)} %copy-done), custom_call_target="tpu_custom_call" | custom-call | tf_op jit(solution)/shard_map/taps_spectrum/pallas_call | solution.py:148
  18.4 1.9 %copy-done.1 = f32[8,512,256]{2,1,0:T(8,128)} copy-done((f32[8,512,256]{2,1,0:T(8,128)}, f32[8,512,256]{2,1,0:T(8,128)S(1)}, u32[]{:S(2)}) %copy-start.1) | copy-done | bytes 4194328
  20.3 19.6 %all-to-all-done.fields_ref = bf16[16,2,128,256]{3,2,1,0:T(8,128)(2,1)S(1)} async-done(((bf16[16,2,128,256]{3,2,1,0:T(8,128)(2,1)}), bf16[16,2,128,256]{3,2,1,0:T(8,128)(2,1)S(1)}, u32[]{:S(2)}, u32[]{:S(2)}) %all-to-all-start) | async-done | bytes 2097184 | tf_op jit(solution)/shard_map/all_to_all | solution.py:321
  39.9 16.9 %transforms.1 = (bf16[16,2,128,256]{3,2,1,0:T(8,128)(2,1)S(1)}, bf16[2048,256]{1,0:T(8,128)(2,1)S(1)}) custom-call(bf16[16,2,128,256]{3,2,1,0:T(8,128)(2,1)S(1)} %all-to-all-done.fields_ref, f32[8,512,256]{2,1,0:T(8,128)} %copy-done.1, bf16[8,512,512]{2,1,0:T(8,128)(2,1)} %constant.70.clone.table_ref.forward_ref, bf16[8,512,512]{2,1,0:T(8,128)(2,1)} %constant.71.clone.inverse_ref), custom_call_target="tpu_custom_call" | custom-call | tf_op jit(solution)/shard_map/transforms/pallas_call | solution.py:254
  56.8 1.3 %copy-done.3 = bf16[16,2,128,256]{3,2,1,0:T(8,128)(2,1)} copy-done((bf16[16,2,128,256]{3,2,1,0:T(8,128)(2,1)}, bf16[16,2,128,256]{3,2,1,0:T(8,128)(2,1)S(1)}, u32[]{:S(2)}) %copy-start.3) | copy-done | bytes 2097176
  58.2 5.5 %all-to-all-start.1 = ((bf16[16,2,128,256]{3,2,1,0:T(8,128)(2,1)}), bf16[16,2,128,256]{3,2,1,0:T(8,128)(2,1)S(1)}, u32[]{:S(2)}, u32[]{:S(2)}) async-start(bf16[16,2,128,256]{3,2,1,0:T(8,128)(2,1)} %copy-done.3), calls=%async_computation.1 | async-start | bytes 4194304 | tf_op jit(solution)/shard_map/all_to_all | solution.py:324
  63.7 0.8 dynamic-slice_bitcast_fusion
  64.5 3.0 %collective-permute-start = (bf16[4,256,256]{2,1,0:T(8,128)(2,1)}, bf16[4,256,256]{2,1,0:T(8,128)(2,1)}, u32[]{:S(2)}, u32[]{:S(2)}) collective-permute-start(bf16[4,256,256]{2,1,0:T(8,128)(2,1)} %dynamic-slice_bitcast_fusion), channel_id=1, source_target_pairs={{0,96},{16,112},{32,64},{48,80},{64,32},{80,48},{96,0},{112,16},{1... | collective-permute-start | bytes 1572872 | tf_op jit(solution)/shard_map/ppermute | solution.py:304
  67.5 12.8 %collective-permute-done = bf16[4,256,256]{2,1,0:T(8,128)(2,1)} collective-permute-done((bf16[4,256,256]{2,1,0:T(8,128)(2,1)}, bf16[4,256,256]{2,1,0:T(8,128)(2,1)}, u32[]{:S(2)}, u32[]{:S(2)}) %collective-permute-start) | collective-permute-done | bytes 524320 | tf_op jit(solution)/shard_map/ppermute | solution.py:304
  80.3 1.1 %convert_add_fusion = f32[4,256,256]{2,1,0:T(8,128)S(1)} fusion(bf16[4,256,256]{2,1,0:T(8,128)(2,1)} %collective-permute-done, bf16[2,4,256,256]{3,2,1,0:T(8,128)(2,1)S(1)} %bitcast.16, s32[]{:T(128)S(6)} %select_n.40), kind=kLoop, calls=%fused_computation | loop fusion | flops 786432 | bytes 2097156 | tf_op jit(solution)/shard_map/add | solution.py:304
  81.5 1.0 copy-done.5
  82.5 0.4 collective-permute-start.1
  82.9 7.6 %collective-permute-done.1 = bf16[2,256,256]{2,1,0:T(8,128)(2,1)S(1)} collective-permute-done((bf16[2,256,256]{2,1,0:T(8,128)(2,1)S(1)}, bf16[2,256,256]{2,1,0:T(8,128)(2,1)S(1)}, u32[]{:S(2)}, u32[]{:S(2)}) %collective-permute-start.1) | collective-permute-done | bytes 262176 | tf_op jit(solution)/shard_map/ppermute | solution.py:304
  90.5 1.1 %bitcast_add_fusion = f32[2,256,256]{2,1,0:T(8,128)S(1)} fusion(bf16[2,256,256]{2,1,0:T(8,128)(2,1)S(1)} %collective-permute-done.1, f32[2,2,256,256]{3,2,1,0:T(8,128)} %bitcast.18, s32[]{:T(128)S(6)} %select_n.44), kind=kLoop, calls=%fused_computation.1 | loop fusion | flops 262144 | bytes 1310724 | tf_op jit(solution)/shard_map/add | solution.py:304
  91.6 2.8 %collective-permute-start.2 = (bf16[256,256]{1,0:T(8,128)(2,1)S(1)}, bf16[256,256]{1,0:T(8,128)(2,1)S(1)}, u32[]{:S(2)}, u32[]{:S(2)}) collective-permute-start(bf16[256,256]{1,0:T(8,128)(2,1)S(1)} %fusion.1), channel_id=1, source_target_pairs={{0,16},{16,0},{32,48},{48,32},{64,80},{80,64},{96,112},{112,96},{1... | collective-permute-start | bytes 393224 | tf_op jit(solution)/shard_map/ppermute | solution.py:304
  94.4 3.7 %collective-permute-done.2 = bf16[256,256]{1,0:T(8,128)(2,1)S(1)} collective-permute-done((bf16[256,256]{1,0:T(8,128)(2,1)S(1)}, bf16[256,256]{1,0:T(8,128)(2,1)S(1)}, u32[]{:S(2)}, u32[]{:S(2)}) %collective-permute-start.2) | collective-permute-done | bytes 131104 | tf_op jit(solution)/shard_map/ppermute | solution.py:304
  98.1 0.7 bitcast_add_fusion.1
  98.9 1.3 %copy-done.4 = bf16[16,2,128,256]{3,2,1,0:T(8,128)(2,1)} copy-done((bf16[16,2,128,256]{3,2,1,0:T(8,128)(2,1)}, bf16[16,2,128,256]{3,2,1,0:T(8,128)(2,1)S(1)}, u32[]{:S(2)}) %copy-start.4) | copy-done | bytes 2097176
  100.2 3.9 %outputs.1 = (bf16[1,128,4096]{2,1,0:T(8,128)(2,1)}, bf16[1,128,4096]{2,1,0:T(8,128)(2,1)}) custom-call(bf16[16,2,128,256]{3,2,1,0:T(8,128)(2,1)} %copy-done.4, bf16[1,128,4096]{2,1,0:T(8,128)(2,1)} %cotangent_ref.3), custom_call_target="tpu_custom_call" | custom-call | tf_op jit(solution)/shard_map/outputs/pallas_call | solution.py:288
  (8 shorter events, 0.1 us)
Async XLA Ops:
  4.7 35.2 %all-to-all-start = ((bf16[16,2,128,256]{3,2,1,0:T(8,128)(2,1)}), bf16[16,2,128,256]{3,2,1,0:T(8,128)(2,1)S(1)}, u32[]{:S(2)}, u32[]{:S(2)}) async-start(bf16[16,2,128,256]{3,2,1,0:T(8,128)(2,1)} %product.1), calls=%async_computation | async-start | bytes 4194304 | tf_op jit(solution)/shard_map/all_to_all | solution.py:321
  11.1 2.2 %copy-start = (bf16[8,512,512]{2,1,0:T(8,128)(2,1)S(1)}, bf16[8,512,512]{2,1,0:T(8,128)(2,1)}, u32[]{:S(2)}) copy-start(bf16[8,512,512]{2,1,0:T(8,128)(2,1)} %constant.70.clone.table_ref.forward_ref) | copy-start | bytes 12582916
  13.3 1.6 %copy-start.2 = (f32[2048,256]{1,0:T(8,128)S(1)}, f32[2048,256]{1,0:T(8,128)}, u32[]{:S(2)}) copy-start(f32[2048,256]{1,0:T(8,128)} %taps_ref.1) | copy-start | bytes 6291460
  18.4 1.9 %copy-start.1 = (f32[8,512,256]{2,1,0:T(8,128)}, f32[8,512,256]{2,1,0:T(8,128)S(1)}, u32[]{:S(2)}) copy-start(f32[8,512,256]{2,1,0:T(8,128)S(1)} %taps_spectrum.1.taps_ref) | copy-start | bytes 12582916
  56.8 1.3 %copy-start.3 = (bf16[16,2,128,256]{3,2,1,0:T(8,128)(2,1)}, bf16[16,2,128,256]{3,2,1,0:T(8,128)(2,1)S(1)}, u32[]{:S(2)}) copy-start(bf16[16,2,128,256]{3,2,1,0:T(8,128)(2,1)S(1)} %get-tuple-element.7) | copy-start | bytes 6291460
  58.2 40.7 %all-to-all-start.1 = ((bf16[16,2,128,256]{3,2,1,0:T(8,128)(2,1)}), bf16[16,2,128,256]{3,2,1,0:T(8,128)(2,1)S(1)}, u32[]{:S(2)}, u32[]{:S(2)}) async-start(bf16[16,2,128,256]{3,2,1,0:T(8,128)(2,1)} %copy-done.3), calls=%async_computation.1 | async-start | bytes 4194304 | tf_op jit(solution)/shard_map/all_to_all | solution.py:324
  64.5 15.8 %collective-permute-start = (bf16[4,256,256]{2,1,0:T(8,128)(2,1)}, bf16[4,256,256]{2,1,0:T(8,128)(2,1)}, u32[]{:S(2)}, u32[]{:S(2)}) collective-permute-start(bf16[4,256,256]{2,1,0:T(8,128)(2,1)} %dynamic-slice_bitcast_fusion), channel_id=1, source_target_pairs={{0,96},{16,112},{32,64},{48,80},{64,32},{80,48},{96,0},{112,16},{1... | collective-permute-start | bytes 1572872 | tf_op jit(solution)/shard_map/ppermute | solution.py:304
  81.5 1.0 copy-start.5
  82.5 8.0 %collective-permute-start.1 = (bf16[2,256,256]{2,1,0:T(8,128)(2,1)S(1)}, bf16[2,256,256]{2,1,0:T(8,128)(2,1)S(1)}, u32[]{:S(2)}, u32[]{:S(2)}) collective-permute-start(bf16[2,256,256]{2,1,0:T(8,128)(2,1)S(1)} %fusion), channel_id=1, source_target_pairs={{0,32},{16,48},{32,0},{48,16},{64,96},{80,112},{96,64},{112,80},{1... | collective-permute-start | bytes 786440 | tf_op jit(solution)/shard_map/ppermute | solution.py:304
  91.6 6.6 %collective-permute-start.2 = (bf16[256,256]{1,0:T(8,128)(2,1)S(1)}, bf16[256,256]{1,0:T(8,128)(2,1)S(1)}, u32[]{:S(2)}, u32[]{:S(2)}) collective-permute-start(bf16[256,256]{1,0:T(8,128)(2,1)S(1)} %fusion.1), channel_id=1, source_target_pairs={{0,16},{16,0},{32,48},{48,32},{64,80},{80,64},{96,112},{112,96},{1... | collective-permute-start | bytes 393224 | tf_op jit(solution)/shard_map/ppermute | solution.py:304
  98.9 1.3 %copy-start.4 = (bf16[16,2,128,256]{3,2,1,0:T(8,128)(2,1)}, bf16[16,2,128,256]{3,2,1,0:T(8,128)(2,1)S(1)}, u32[]{:S(2)}) copy-start(bf16[16,2,128,256]{3,2,1,0:T(8,128)(2,1)S(1)} %all-to-all-done.1.back_ref) | copy-start | bytes 6291460

commit v2 on v1

v2 whole, which is shorter than its diff:
```python
import functools
import math

import jax
import jax.numpy as jnp
import ml_dtypes
import numpy as np
from jax import lax
from jax.experimental import pallas as pl
from jax.experimental.pallas import tpu as pltpu
from jax.sharding import PartitionSpec as P

F32 = jnp.float32
BF16 = jnp.bfloat16
RADIX = 32
INNER = 128
TOTAL = RADIX * INNER
BLOCKS = RADIX // 2
ROOT_HALF = math.sqrt(0.5)
COS_EIGHTH = math.cos(math.pi / 8)
SIN_EIGHTH = math.sin(math.pi / 8)
TURNS = [(math.cos(math.pi * k / 16), math.sin(math.pi * k / 16)) for k in (1, 3, 5, 7)]
CHANNELS = 256
ROWS = 16
LANES = 128


def section_tables():
    column = np.arange(INNER)[None, :]
    forward = np.zeros((BLOCKS, 2 * INNER, 2 * INNER))
    half = INNER // 2
    row = np.arange(half)[:, None]
    for section in range(2):
        angle = 2 * np.pi * ((column * (RADIX * row + BLOCKS * section)) % TOTAL) / TOTAL
        place = slice(section * INNER, (section + 1) * INNER)
        forward[0, section * half : (section + 1) * half, place] = np.cos(angle)
        forward[0, INNER + section * half : INNER + (section + 1) * half, place] = -np.sin(angle)
    forward[0, INNER, :INNER] = np.cos(np.pi * column[0])
    row = np.arange(INNER)[:, None]
    for j in range(1, BLOCKS):
        angle = 2 * np.pi * ((column * (RADIX * row + j)) % TOTAL) / TOTAL
        forward[j] = np.block([[np.cos(angle), np.sin(angle)], [-np.sin(angle), np.cos(angle)]])
    return forward.astype(ml_dtypes.bfloat16)


def half_sections(y0, y2, y4, y6):
    t, q = ROOT_HALF * (y2 - y6), ROOT_HALF * (y2 + y6)
    return (y0 + t, -(y4 + q)), (y0 - t, y4 - q)


def odd_sections(x):
    x0, x1, x2, x3, x4, x5, x6, x7 = x
    (e1r, e1i), (e3r, e3i) = half_sections(x0, x2, x4, x6)
    (o1r, o1i), (o3r, o3i) = half_sections(x1, x3, x5, x7)
    m1r, m1i = COS_EIGHTH * o1r + SIN_EIGHTH * o1i, COS_EIGHTH * o1i - SIN_EIGHTH * o1r
    m3r, m3i = SIN_EIGHTH * o3r + COS_EIGHTH * o3i, SIN_EIGHTH * o3i - COS_EIGHTH * o3r
    return (e1r + m1r, e1i + m1i), (e3r + m3r, e3i + m3i), (e3r - m3r, m3i - e3i), (e1r - m1r, m1i - e1i)


def sections(x):
    a = [x[n] + x[n + 8] for n in range(8)]
    b = [x[n] - x[n + 8] for n in range(8)]
    c = [a[n] + a[n + 4] for n in range(4)]
    d = [a[n] - a[n + 4] for n in range(4)]
    even, odd = c[0] + c[2], c[1] + c[3]
    t, q = ROOT_HALF * (d[1] - d[3]), ROOT_HALF * (d[1] + d[3])
    out = [None] * 16
    out[0] = (even + odd, even - odd)
    out[4] = (d[0] + t, -(d[2] + q))
    out[8] = (c[0] - c[2], c[3] - c[1])
    out[12] = (d[0] - t, d[2] - q)
    out[2], out[6], out[10], out[14] = odd_sections(b)
    pairs = zip((1, 3, 5, 7), TURNS, odd_sections(x[0::2]), odd_sections(x[1::2]))
    for k, (cos, sin), (er, ei), (tr, ti) in pairs:
        mr, mi = cos * tr + sin * ti, cos * ti - sin * tr
        out[k] = (er + mr, ei + mi)
        out[16 - k] = (er - mr, mi - ei)
    return out


def half_gather(e1r, e1i, e3r, e3i):
    t, w = ROOT_HALF * (e1r - e3r), ROOT_HALF * (e1i + e3i)
    return e1r + e3r, t - w, e3i - e1i, -(t + w)


def odd_gather(v1, v3, v5, v7):
    e1r, e1i, m1r, m1i = v1[0] + v7[0], v1[1] - v7[1], v1[0] - v7[0], v1[1] + v7[1]
    e3r, e3i, m3r, m3i = v3[0] + v5[0], v3[1] - v5[1], v3[0] - v5[0], v3[1] + v5[1]
    o1r, o1i = COS_EIGHTH * m1r - SIN_EIGHTH * m1i, SIN_EIGHTH * m1r + COS_EIGHTH * m1i
    o3r, o3i = SIN_EIGHTH * m3r - COS_EIGHTH * m3i, COS_EIGHTH * m3r + SIN_EIGHTH * m3i
    y0, y2, y4, y6 = half_gather(e1r, e1i, e3r, e3i)
    y1, y3, y5, y7 = half_gather(o1r, o1i, o3r, o3i)
    return [y0, y1, y2, y3, y4, y5, y6, y7]


def gather_sections(v):
    even, odd = v[0][0] + v[0][1], v[0][0] - v[0][1]
    c = [even + v[8][0], odd - v[8][1], even - v[8][0], odd + v[8][1]]
    t, w = ROOT_HALF * (v[4][0] - v[12][0]), ROOT_HALF * (v[4][1] + v[12][1])
    d = [v[4][0] + v[12][0], t - w, v[12][1] - v[4][1], -(t + w)]
    a = [c[n] + d[n] for n in range(4)] + [c[n] - d[n] for n in range(4)]
    b = odd_gather(v[2], v[6], v[10], v[14])
    straight, turned = [], []
    for k, (cos, sin) in zip((1, 3, 5, 7), TURNS):
        (pr, pi), (qr, qi) = v[k], v[16 - k]
        mr, mi = pr - qr, pi + qi
        straight.append((pr + qr, pi - qi))
        turned.append((cos * mr - sin * mi, sin * mr + cos * mi))
    ye, yo = odd_gather(*straight), odd_gather(*turned)
    y = [part for both in zip(ye, yo) for part in both]
    return [a[n] + b[n] + y[n] for n in range(8)] + [a[n] - b[n] + y[n + 8] for n in range(8)]


HBM = pl.BlockSpec(memory_space=pltpu.HBM)
VMEM = pl.BlockSpec(memory_space=pltpu.VMEM)
PARTS = 4


def product_kernel(signal_ref, gate_ref, cotangent_ref, out_ref, fields, products, in_sems, out_sems):
    each = fields.shape[2] // PARTS
    pieces = each // CHANNELS
    loads = []
    for part in range(PARTS):
        lanes = pl.ds(part * each, each)
        for field, ref in enumerate((gate_ref, cotangent_ref, signal_ref)):
            loads.append(pltpu.make_async_copy(ref.at[0, :, lanes], fields.at[field, :, lanes], in_sems.at[part, field]))
            loads[-1].start()
    stores = []
    for part in range(PARTS):
        for field in range(2):
            loads[3 * part + field].wait()
        for piece in range(part * pieces, (part + 1) * pieces):
            lanes = pl.ds(piece * CHANNELS, CHANNELS)
            products[piece] = (fields[1, :, lanes].astype(F32) * fields[0, :, lanes].astype(F32)).astype(BF16)
        whole = pl.ds(part * pieces, pieces)
        stores.append(pltpu.make_async_copy(products.at[whole], out_ref.at[whole, 1], out_sems.at[part]))
        stores[-1].start()
        loads[3 * part + 2].wait()
        for piece in range(part * pieces, (part + 1) * pieces):
            lanes = pl.ds(piece * CHANNELS, CHANNELS)
            stores.append(pltpu.make_async_copy(fields.at[2, :, lanes], out_ref.at[piece, 0], out_sems.at[PARTS + piece]))
            stores[-1].start()
    for store in stores:
        store.wait()


def send_fields(signal, gate, cotangent, count):
    rows, width = signal.shape[1:]
    return pl.pallas_call(
        product_kernel,
        in_specs=[HBM] * 3,
        out_specs=HBM,
        out_shape=jax.ShapeDtypeStruct((count, 2, rows, width // count), BF16),
        scratch_shapes=[
            pltpu.VMEM((3, rows, width), BF16),
            pltpu.VMEM((count, rows, width // count), BF16),
            pltpu.SemaphoreType.DMA((PARTS, 3)),
            pltpu.SemaphoreType.DMA((PARTS + count,)),
        ],
        compiler_params=pltpu.CompilerParams(vmem_limit_bytes=60 << 20),
        name="product",
    )(signal, gate, cotangent)


def chunk_of(i):
    start = pl.multiple_of((i // 2) * ROWS, ROWS)
    lanes = pl.ds(pl.multiple_of((i % 2) * LANES, LANES), LANES)
    return pl.ds(start, ROWS), pl.ds(pl.multiple_of(INNER + start, ROWS), ROWS), lanes


def split_chunk(i, sections_ref, load):
    rows, low, lanes = chunk_of(i)
    x = [load(n, rows, lanes) for n in range(RADIX // 2)]
    for j, (real, imag) in enumerate(sections(x)):
        sections_ref[j, rows, lanes] = real.astype(BF16)
        sections_ref[j, low, lanes] = imag.astype(BF16)


def gather_chunk(i, parts_ref, store):
    rows, low, lanes = chunk_of(i)
    v = [(parts_ref[j, rows, lanes], parts_ref[j, low, lanes]) for j in range(BLOCKS)]
    for n, y in enumerate(gather_sections(v)):
        store(n, rows, lanes, y)


def repeat(step):
    def body(i, _):
        step(i)
        return 0

    lax.fori_loop(0, BLOCKS, body, 0, unroll=True)


def taps_kernel(scale, taps_ref, forward_ref, out_ref, sections_ref):
    def load(n, rows, lanes):
        return taps_ref[pl.ds(pl.multiple_of(n * INNER + rows.start, ROWS), ROWS), lanes] * scale

    repeat(lambda i: split_chunk(i, sections_ref, load))
    for j in range(BLOCKS):
        out_ref[j] = jnp.dot(forward_ref[j], sections_ref[j], preferred_element_type=F32).astype(BF16)


def taps_spectrum(taps, forward):
    length, width = taps.shape
    return pl.pallas_call(
        functools.partial(taps_kernel, 2.0 / TOTAL / math.sqrt(length)),
        in_specs=[VMEM, VMEM],
        out_specs=VMEM,
        out_shape=jax.ShapeDtypeStruct((BLOCKS, 2 * INNER, width), BF16),
        scratch_shapes=[pltpu.VMEM((BLOCKS, 2 * INNER, width), BF16)],
        compiler_params=pltpu.CompilerParams(vmem_limit_bytes=24 << 20),
        name="taps_spectrum",
    )(taps, forward)


def multiply_spectra(left, right, conjugate, lone):
    lr, li, rr, ri = left[:INNER], left[INNER:], right[:INNER], right[INNER:]
    if conjugate:
        pr, pi = lr * rr + li * ri, lr * ri - li * rr
    else:
        pr, pi = lr * rr - li * ri, lr * ri + li * rr
    if lone:
        first = lax.broadcasted_iota(jnp.int32, pr.shape, 0) == 0
        pr, pi = jnp.where(first, 0.5 * lr * rr, pr), jnp.where(first, 0.5 * li * ri, pi)
    return jnp.concatenate([pr.astype(BF16), pi.astype(BF16)], axis=0)


def transforms_kernel(
    scale,
    fields_hbm,
    taps_hbm,
    forward_hbm,
    back_ref,
    term_0_ref,
    term_1_ref,
    term_2_ref,
    term_3_ref,
    fields_ref,
    taps_ref,
    forward_ref,
    sections_ref,
    signal_ref,
    spectra_ref,
    parts_ref,
    back_buf,
    term_buf,
    load_sems,
    store_sems,
):
    loads = []

    def load(hbm, vmem, pieces):
        each = hbm.shape[0] // pieces
        for piece in range(pieces):
            part = pl.ds(piece * each, each)
            loads.append(pltpu.make_async_copy(hbm.at[part], vmem.at[part], load_sems.at[len(loads)]))
            loads[-1].start()
        return loads[-pieces:]

    def finish(copies):
        for copy in copies:
            copy.wait()

    stores = []

    def store_copy(source, target):
        stores.append(pltpu.make_async_copy(source, target, store_sems.at[len(stores)]))
        stores[-1].start()

    def split(i, field):
        split_chunk(
            i, sections_ref.at[field], lambda n, rows, lanes: fields_ref[field, n, rows, lanes].astype(F32)
        )

    def gather(i, out):
        def store(n, rows, lanes, y):
            if out == 2:
                place = pl.ds(pl.multiple_of((n % 2) * INNER + rows.start, ROWS), ROWS)
                term_buf[n // 4, (n // 2) % 2, place, lanes] = (y * scale).astype(BF16)
            else:
                back_buf[out, n, rows, lanes] = y.astype(BF16)

        gather_chunk(i, parts_ref.at[out], store)

    def forward(j, field):
        return jnp.dot(forward_ref[j], sections_ref[field, j], preferred_element_type=F32)

    def inverse(j, out):
        parts_ref[out, j] = lax.dot_general(
            forward_ref[j], spectra_ref[out, j], (((0,), (0,)), ((), ())), preferred_element_type=F32
        )

    def multiply(j, lone):
        product, taps, signal = forward(j, 1), taps_ref[j].astype(F32), signal_ref[j]
        spectra_ref[0, j] = multiply_spectra(taps, product, True, lone)
        spectra_ref[1, j] = multiply_spectra(taps, signal, False, lone)
        spectra_ref[2, j] = multiply_spectra(signal, product, True, lone)

    def second_split(i):
        split(i, 1)
        signal_ref[i] = forward(i, 0)

    def first_gather(i):
        gather(i, 2)
        inverse(i, 0)

    def second_gather(i):
        gather(i, 0)
        inverse(i, 1)

    first_load = load(fields_hbm.at[:, 0], fields_ref.at[0], 4)
    second_load = load(fields_hbm.at[:, 1], fields_ref.at[1], 2)
    forward_load = load(forward_hbm, forward_ref, 2)
    taps_load = load(taps_hbm, taps_ref, 2)
    finish(first_load)
    repeat(lambda i: split(i, 0))
    finish(forward_load + second_load)
    repeat(second_split)
    finish(taps_load)
    for j in range(BLOCKS):
        multiply(j, j == 0)
    repeat(lambda i: inverse(i, 2))
    repeat(first_gather)
    column, side = lax.axis_index("dp") // 2, lax.axis_index("dp") % 2
    for turn, ref in enumerate((term_0_ref, term_1_ref, term_2_ref, term_3_ref)):
        for half in range(2):
            store_copy(term_buf.at[(column + turn) % 4, (side + half) % 2], ref.at[half])
    repeat(second_gather)
    store_copy(back_buf.at[0], back_ref.at[:, 0])
    for quarter in range(4):
        for i in range(quarter * 4, quarter * 4 + 4):
            gather(i, 1)
        rows = pl.ds(quarter * 2 * ROWS, 2 * ROWS)
        store_copy(back_buf.at[1, :, rows], back_ref.at[:, 1, rows])
    finish(stores)


def transforms(fields, taps_spec, forward):
    count, _, rows, width = fields.shape
    length = count * rows
    block = (2 * INNER, width)
    return pl.pallas_call(
        functools.partial(transforms_kernel, 2.0 / TOTAL / math.sqrt(length)),
        in_specs=[HBM] * 3,
        out_specs=[HBM] * 5,
        out_shape=[jax.ShapeDtypeStruct(fields.shape, BF16)]
        + [jax.ShapeDtypeStruct((2, length // 8, width), BF16)] * 4,
        scratch_shapes=[
            pltpu.VMEM((2, count, rows, width), BF16),
            pltpu.VMEM((BLOCKS,) + block, BF16),
            pltpu.VMEM(forward.shape, BF16),
            pltpu.VMEM((2, BLOCKS) + block, BF16),
            pltpu.VMEM((BLOCKS,) + block, F32),
            pltpu.VMEM((3, BLOCKS) + block, BF16),
            pltpu.VMEM((3, BLOCKS) + block, F32),
            pltpu.VMEM((2, count, rows, width), BF16),
            pltpu.VMEM((4, 2, length // 8, width), BF16),
            pltpu.SemaphoreType.DMA((16,)),
            pltpu.SemaphoreType.DMA((13,)),
        ],
        compiler_params=pltpu.CompilerParams(vmem_limit_bytes=61 << 20),
        name="transforms",
    )(fields, taps_spec, forward)


def outputs_kernel(back_ref, cotangent_ref, signal_grad_ref, gate_grad_ref, gate_buf, sems):
    count = back_ref.shape[0]
    pieces = count // PARTS
    stores = []
    for piece in range(count):
        lanes = pl.ds(piece * CHANNELS, CHANNELS)
        stores.append(pltpu.make_async_copy(back_ref.at[piece, 0], signal_grad_ref.at[0, :, lanes], sems.at[piece]))
        stores[-1].start()
    for part in range(PARTS):
        for piece in range(part * pieces, (part + 1) * pieces):
            lanes = pl.ds(piece * CHANNELS, CHANNELS)
            gate_buf[:, lanes] = (cotangent_ref[0, :, lanes].astype(F32) * back_ref[piece, 1].astype(F32)).astype(BF16)
        lanes = pl.ds(part * pieces * CHANNELS, pieces * CHANNELS)
        stores.append(pltpu.make_async_copy(gate_buf.at[:, lanes], gate_grad_ref.at[0, :, lanes], sems.at[count + part]))
        stores[-1].start()
    for store in stores:
        store.wait()


def place_outputs(back, cotangent):
    return pl.pallas_call(
        outputs_kernel,
        in_specs=[VMEM, VMEM],
        out_specs=[HBM, HBM],
        out_shape=[jax.ShapeDtypeStruct(cotangent.shape, BF16)] * 2,
        scratch_shapes=[
            pltpu.VMEM(cotangent.shape[1:], BF16),
            pltpu.SemaphoreType.DMA((back.shape[0] + PARTS,)),
        ],
        compiler_params=pltpu.CompilerParams(vmem_limit_bytes=12 << 20),
        name="outputs",
    )(back, cotangent)


def sum_over_sequences(quarters):
    devices = lax.axis_size("dp")
    terms = [quarters[0]]
    for turn in (2, 1, 3):
        terms.append(lax.ppermute(quarters[turn], "dp", [(d, (d + 2 * turn) % devices) for d in range(devices)]))
    keep, away = (sum(term[half].astype(F32) for term in terms) for half in range(2))
    return keep, lax.ppermute(away.astype(BF16), "dp", [(d, d ^ 1) for d in range(devices)])


def local(signal, gate, cotangent, filter_taps):
    count = lax.axis_size("ctx")
    forward = section_tables()
    fields = lax.all_to_all(send_fields(signal, gate, cotangent, count), "ctx", 0, 0, tiled=True)
    taps_spec = taps_spectrum(filter_taps, forward)
    back, *quarters = transforms(fields, taps_spec, forward)
    back = lax.all_to_all(back, "ctx", 0, 0, tiled=True)
    keep, other = sum_over_sequences(quarters)
    signal_grad, gate_grad = place_outputs(back, cotangent)
    signal_grad, other = lax.optimization_barrier((signal_grad, other))
    return (signal_grad, gate_grad, keep + other.astype(F32))


def solution(mesh):
    in_specs = (P("dp", "ctx", None), P("dp", "ctx", None), P("dp", "ctx", None), P(None, "ctx"))
    out_specs = (P("dp", "ctx", None), P("dp", "ctx", None), P("dp", "ctx"))
    return jax.shard_map(local, mesh=mesh, in_specs=in_specs, out_specs=out_specs, check_vma=False)
```

time: 105 us -> 90.5 us (0.86)
  the two profiles are of different devices: /device:TPU:0 before, /device:TPU:40 now
where the time goes in v2:
time: 90.5 us; the launch traced here: 90.2 us
  waiting for transfers between devices  46.5 us (51%)
  starting transfers between devices  20.6 us (23%)
  Pallas kernels  17.8 us (20%)
  local copies, waits for them, and re-layouts  2.97 us (3%)
  other arithmetic  1.61 us (2%)
    all_to_all x1, waiting for transfers between devices, local(): lax.all_to_all(send_fields(signal, gate, cotangent, count), 'ctx', 0, 0,...  22.5 us
    ppermute x3, waiting for transfers between devices, sum_over_sequences(): lax.ppermute(quarters[turn], 'dp', [(d, (d + 2 * turn) % devices) for d i...  11.5 us
    pallas_call x1, Pallas kernels, transforms(): pl.pallas_call(functools.partial(transforms_kernel, 2.0 / TOTAL / math.sq...  11.3 us
    all_to_all x1, waiting for transfers between devices, local(): back = lax.all_to_all(back, 'ctx', 0, 0, tiled=True)  8.5 us
    all_to_all x1, starting transfers between devices, local(): back = lax.all_to_all(back, 'ctx', 0, 0, tiled=True)  7.01 us
    all_to_all x1, starting transfers between devices, local(): lax.all_to_all(send_fields(signal, gate, cotangent, count), 'ctx', 0, 0,...  6.51 us
    ppermute x3, starting transfers between devices, sum_over_sequences(): lax.ppermute(quarters[turn], 'dp', [(d, (d + 2 * turn) % devices) for d i...  4.32 us
    ppermute x1, waiting for transfers between devices, sum_over_sequences(): lax.ppermute(away.astype(BF16), 'dp', [(d, d ^ 1) for d in range(devices)])  3.93 us
  transfers between devices with their start and end apart: 6, of which 5 were waited for; matrix products, arithmetic and copies ran while one was open for 1% of the time, Pallas kernels for 4%

profile of v2, /device:TPU:40, one launch (start us, length us, event | category | flops | bytes accessed | tf_op | source)
XLA Modules:
  0.0 90.2 jit_solution(1474273799612253434)
XLA Ops:
  0.6 2.9 %product.1 = bf16[16,2,128,256]{3,2,1,0:T(8,128)(2,1)} custom-call(bf16[1,128,4096]{2,1,0:T(8,128)(2,1)} %signal_ref.1, bf16[1,128,4096]{2,1,0:T(8,128)(2,1)} %gate_ref.1, bf16[1,128,4096]{2,1,0:T(8,128)(2,1)} %cotangent_ref.3), custom_call_target="tpu_custom_call" | custom-call | tf_op jit(solution)/shard_map/product/pallas_call | solution.py:149
  3.5 0.0 copy-start
  3.6 6.5 %all-to-all-start = ((bf16[16,2,128,256]{3,2,1,0:T(8,128)(2,1)}), bf16[16,2,128,256]{3,2,1,0:T(8,128)(2,1)}, u32[]{:S(2)}, u32[]{:S(2)}) async-start(bf16[16,2,128,256]{3,2,1,0:T(8,128)(2,1)} %product.1), calls=%async_computation | async-start | bytes 4194304 | tf_op jit(solution)/shard_map/all_to_all | solution.py:412
  10.1 0.0 copy-start.3
  10.1 1.6 %copy-done.3 = f32[2048,256]{1,0:T(8,128)S(1)} copy-done((f32[2048,256]{1,0:T(8,128)S(1)}, f32[2048,256]{1,0:T(8,128)}, u32[]{:S(2)}) %copy-start.3) | copy-done | bytes 2097176
  11.7 2.1 %taps_spectrum.1.taps_hbm = bf16[16,256,256]{2,1,0:T(8,128)(2,1)S(1)} custom-call(f32[2048,256]{1,0:T(8,128)S(1)} %copy-done.3, bf16[16,256,256]{2,1,0:T(8,128)(2,1)S(1)} %copy-done), custom_call_target="tpu_custom_call" | custom-call | tf_op jit(solution)/shard_map/taps_spectrum/pallas_call | solution.py:205
  13.7 1.3 %copy-done.1 = bf16[16,256,256]{2,1,0:T(8,128)(2,1)} copy-done((bf16[16,256,256]{2,1,0:T(8,128)(2,1)}, bf16[16,256,256]{2,1,0:T(8,128)(2,1)S(1)}, u32[]{:S(2)}) %copy-start.1) | copy-done | bytes 2097176
  15.1 22.5 %all-to-all-done.fields_hbm = bf16[16,2,128,256]{3,2,1,0:T(8,128)(2,1)} async-done(((bf16[16,2,128,256]{3,2,1,0:T(8,128)(2,1)}), bf16[16,2,128,256]{3,2,1,0:T(8,128)(2,1)}, u32[]{:S(2)}, u32[]{:S(2)}) %all-to-all-start) | async-done | bytes 2097184 | tf_op jit(solution)/shard_map/all_to_all | solution.py:412
  37.6 11.3 %transforms.1 = (bf16[16,2,128,256]{3,2,1,0:T(8,128)(2,1)}, bf16[2,256,256]{2,1,0:T(8,128)(2,1)}, bf16[2,256,256]{2,1,0:T(8,128)(2,1)}, bf16[2,256,256]{2,1,0:T(8,128)(2,1)}, bf16[2,256,256]{2,1,0:T(8,128)(2,1)}) custom-call(bf16[16,2,128,256]{3,2,1,0:T(8,128)(2,1)} %all-to-all-done.fields_hbm, bf16[16,256,256]{2,1,0:T(8,128)(2,1)} %copy-done.1, ...), custom_call_target="tpu_custom_call" | custom-call | tf_op jit(solution)/shard_map/transforms/pallas_call | solution.py:342
  48.9 0.0 copy-start.4
  48.9 0.0 copy-start.2
  48.9 7.0 %all-to-all-start.1 = ((bf16[16,2,128,256]{3,2,1,0:T(8,128)(2,1)}), bf16[16,2,128,256]{3,2,1,0:T(8,128)(2,1)S(1)}, u32[]{:S(2)}, u32[]{:S(2)}) async-start(bf16[16,2,128,256]{3,2,1,0:T(8,128)(2,1)} %get-tuple-element.12), calls=%async_computation.1 | async-start | bytes 4194304 | tf_op jit(solution)/shard_map/all_to_all | solution.py:415
  56.0 2.3 %collective-permute-start = (bf16[2,256,256]{2,1,0:T(8,128)(2,1)}, bf16[2,256,256]{2,1,0:T(8,128)(2,1)S(1)}, u32[]{:S(2)}, u32[]{:S(2)}) collective-permute-start(bf16[2,256,256]{2,1,0:T(8,128)(2,1)} %get-tuple-element.15), channel_id=1, source_target_pairs={{0,64},{16,80},{32,96},{48,112},{64,0},{80,16},{96,32},{112,48},{1... | collective-permute-start | bytes 786440 | tf_op jit(solution)/shard_map/ppermute | solution.py:404
  58.3 0.0 collective-permute-start.1
  58.3 2.0 %collective-permute-start.2 = (bf16[2,256,256]{2,1,0:T(8,128)(2,1)}, bf16[2,256,256]{2,1,0:T(8,128)(2,1)S(1)}, u32[]{:S(2)}, u32[]{:S(2)}) collective-permute-start(bf16[2,256,256]{2,1,0:T(8,128)(2,1)} %get-tuple-element.17), channel_id=1, source_target_pairs={{0,96},{16,112},{32,0},{48,16},{64,32},{80,48},{96,64},{112,80},{1... | collective-permute-start | bytes 786440 | tf_op jit(solution)/shard_map/ppermute | solution.py:404
  60.3 6.6 %collective-permute-done = bf16[2,256,256]{2,1,0:T(8,128)(2,1)S(1)} collective-permute-done((bf16[2,256,256]{2,1,0:T(8,128)(2,1)}, bf16[2,256,256]{2,1,0:T(8,128)(2,1)S(1)}, u32[]{:S(2)}, u32[]{:S(2)}) %collective-permute-start) | collective-permute-done | bytes 262176 | tf_op jit(solution)/shard_map/ppermute | solution.py:404
  66.9 4.9 %collective-permute-done.1 = bf16[2,256,256]{2,1,0:T(8,128)(2,1)S(1)} collective-permute-done((bf16[2,256,256]{2,1,0:T(8,128)(2,1)}, bf16[2,256,256]{2,1,0:T(8,128)(2,1)S(1)}, u32[]{:S(2)}, u32[]{:S(2)}) %collective-permute-start.1) | collective-permute-done | bytes 262176 | tf_op jit(solution)/shard_map/ppermute | solution.py:404
  71.8 0.0 collective-permute-done.2
  71.8 0.8 fusion
  72.6 2.8 %collective-permute-start.3 = (bf16[256,256]{1,0:T(8,128)(2,1)}, bf16[256,256]{1,0:T(8,128)(2,1)S(1)}, u32[]{:S(2)}, u32[]{:S(2)}) collective-permute-start(bf16[256,256]{1,0:T(8,128)(2,1)} %fusion), channel_id=1, source_target_pairs={{0,16},{16,0},{32,48},{48,32},{64,80},{80,64},{96,112},{112,96},{1... | collective-permute-start | bytes 393224 | tf_op jit(solution)/shard_map/ppermute | solution.py:406
  75.5 8.5 %all-to-all-done.1.back_ref = bf16[16,2,128,256]{3,2,1,0:T(8,128)(2,1)S(1)} async-done(((bf16[16,2,128,256]{3,2,1,0:T(8,128)(2,1)}), bf16[16,2,128,256]{3,2,1,0:T(8,128)(2,1)S(1)}, u32[]{:S(2)}, u32[]{:S(2)}) %all-to-all-start.1) | async-done | bytes 2097184 | tf_op jit(solution)/shard_map/all_to_all | solution.py:415
  84.0 1.5 %outputs.1 = (bf16[1,128,4096]{2,1,0:T(8,128)(2,1)}, bf16[1,128,4096]{2,1,0:T(8,128)(2,1)}) custom-call(bf16[16,2,128,256]{3,2,1,0:T(8,128)(2,1)S(1)} %all-to-all-done.1.back_ref, bf16[1,128,4096]{2,1,0:T(8,128)(2,1)S(1)} %copy-done.2), custom_call_target="tpu_custom_call" | custom-call | tf_op jit(solution)/shard_map/outputs/pallas_call | solution.py:386
  85.5 3.9 %collective-permute-done.3 = bf16[256,256]{1,0:T(8,128)(2,1)S(1)} collective-permute-done((bf16[256,256]{1,0:T(8,128)(2,1)}, bf16[256,256]{1,0:T(8,128)(2,1)S(1)}, u32[]{:S(2)}, u32[]{:S(2)}) %collective-permute-start.3) | collective-permute-done | bytes 131104 | tf_op jit(solution)/shard_map/ppermute | solution.py:406
  89.4 0.8 bitcast_add_fusion
  (16 shorter events, 0.0 us)
Async XLA Ops:
  3.5 6.5 %copy-start = (bf16[16,256,256]{2,1,0:T(8,128)(2,1)S(1)}, bf16[16,256,256]{2,1,0:T(8,128)(2,1)}, u32[]{:S(2)}) copy-start(bf16[16,256,256]{2,1,0:T(8,128)(2,1)} %constant.2.clone.forward_ref.forward_hbm) | copy-start | bytes 6291460
  3.6 34.0 %all-to-all-start = ((bf16[16,2,128,256]{3,2,1,0:T(8,128)(2,1)}), bf16[16,2,128,256]{3,2,1,0:T(8,128)(2,1)}, u32[]{:S(2)}, u32[]{:S(2)}) async-start(bf16[16,2,128,256]{3,2,1,0:T(8,128)(2,1)} %product.1), calls=%async_computation | async-start | bytes 4194304 | tf_op jit(solution)/shard_map/all_to_all | solution.py:412
  10.1 1.6 %copy-start.3 = (f32[2048,256]{1,0:T(8,128)S(1)}, f32[2048,256]{1,0:T(8,128)}, u32[]{:S(2)}) copy-start(f32[2048,256]{1,0:T(8,128)} %taps_ref.1) | copy-start | bytes 6291460
  13.7 1.4 %copy-start.1 = (bf16[16,256,256]{2,1,0:T(8,128)(2,1)}, bf16[16,256,256]{2,1,0:T(8,128)(2,1)S(1)}, u32[]{:S(2)}) copy-start(bf16[16,256,256]{2,1,0:T(8,128)(2,1)S(1)} %taps_spectrum.1.taps_hbm) | copy-start | bytes 6291460
  48.9 22.9 %copy-start.4 = (bf16[2,256,256]{2,1,0:T(8,128)(2,1)S(1)}, bf16[2,256,256]{2,1,0:T(8,128)(2,1)}, u32[]{:S(2)}) copy-start(bf16[2,256,256]{2,1,0:T(8,128)(2,1)} %get-tuple-element.14) | copy-start | bytes 786436
  48.9 35.0 %copy-start.2 = (bf16[1,128,4096]{2,1,0:T(8,128)(2,1)S(1)}, bf16[1,128,4096]{2,1,0:T(8,128)(2,1)}, u32[]{:S(2)}) copy-start(bf16[1,128,4096]{2,1,0:T(8,128)(2,1)} %cotangent_ref.3) | copy-start | bytes 3145732
  48.9 35.0 %all-to-all-start.1 = ((bf16[16,2,128,256]{3,2,1,0:T(8,128)(2,1)}), bf16[16,2,128,256]{3,2,1,0:T(8,128)(2,1)S(1)}, u32[]{:S(2)}, u32[]{:S(2)}) async-start(bf16[16,2,128,256]{3,2,1,0:T(8,128)(2,1)} %get-tuple-element.12), calls=%async_computation.1 | async-start | bytes 4194304 | tf_op jit(solution)/shard_map/all_to_all | solution.py:415
  56.0 10.9 %collective-permute-start = (bf16[2,256,256]{2,1,0:T(8,128)(2,1)}, bf16[2,256,256]{2,1,0:T(8,128)(2,1)S(1)}, u32[]{:S(2)}, u32[]{:S(2)}) collective-permute-start(bf16[2,256,256]{2,1,0:T(8,128)(2,1)} %get-tuple-element.15), channel_id=1, source_target_pairs={{0,64},{16,80},{32,96},{48,112},{64,0},{80,16},{96,32},{112,48},{1... | collective-permute-start | bytes 786440 | tf_op jit(solution)/shard_map/ppermute | solution.py:404
  58.3 13.6 %collective-permute-start.1 = (bf16[2,256,256]{2,1,0:T(8,128)(2,1)}, bf16[2,256,256]{2,1,0:T(8,128)(2,1)S(1)}, u32[]{:S(2)}, u32[]{:S(2)}) collective-permute-start(bf16[2,256,256]{2,1,0:T(8,128)(2,1)} %get-tuple-element.16), channel_id=1, source_target_pairs={{0,32},{16,48},{32,64},{48,80},{64,96},{80,112},{96,0},{112,16},{1... | collective-permute-start | bytes 786440 | tf_op jit(solution)/shard_map/ppermute | solution.py:404
  58.3 13.6 %collective-permute-start.2 = (bf16[2,256,256]{2,1,0:T(8,128)(2,1)}, bf16[2,256,256]{2,1,0:T(8,128)(2,1)S(1)}, u32[]{:S(2)}, u32[]{:S(2)}) collective-permute-start(bf16[2,256,256]{2,1,0:T(8,128)(2,1)} %get-tuple-element.17), channel_id=1, source_target_pairs={{0,96},{16,112},{32,0},{48,16},{64,32},{80,48},{96,64},{112,80},{1... | collective-permute-start | bytes 786440 | tf_op jit(solution)/shard_map/ppermute | solution.py:404
  66.9 5.8 %copy-start.5 = (bf16[2,256,256]{2,1,0:T(8,128)(2,1)}, bf16[2,256,256]{2,1,0:T(8,128)(2,1)S(1)}, u32[]{:S(2)}) copy-start(bf16[2,256,256]{2,1,0:T(8,128)(2,1)S(1)} %collective-permute-done) | copy-start | bytes 786436
  71.8 0.8 copy-start.7
  71.8 0.8 copy-start.9
  72.6 16.7 %collective-permute-start.3 = (bf16[256,256]{1,0:T(8,128)(2,1)}, bf16[256,256]{1,0:T(8,128)(2,1)S(1)}, u32[]{:S(2)}, u32[]{:S(2)}) collective-permute-start(bf16[256,256]{1,0:T(8,128)(2,1)} %fusion), channel_id=1, source_target_pairs={{0,16},{16,0},{32,48},{48,32},{64,80},{80,64},{96,112},{112,96},{1... | collective-permute-start | bytes 393224 | tf_op jit(solution)/shard_map/ppermute | solution.py:406
  84.0 5.4 %copy-start.6 = (bf16[2,256,256]{2,1,0:T(8,128)(2,1)S(1)}, bf16[2,256,256]{2,1,0:T(8,128)(2,1)}, u32[]{:S(2)}) copy-start(bf16[2,256,256]{2,1,0:T(8,128)(2,1)} %copy-done.5) | copy-start | bytes 786436
  84.0 5.4 %copy-start.8 = (bf16[2,256,256]{2,1,0:T(8,128)(2,1)S(1)}, bf16[2,256,256]{2,1,0:T(8,128)(2,1)}, u32[]{:S(2)}) copy-start(bf16[2,256,256]{2,1,0:T(8,128)(2,1)} %copy-done.7) | copy-start | bytes 786436
  84.0 5.4 %copy-start.10 = (bf16[2,256,256]{2,1,0:T(8,128)(2,1)S(1)}, bf16[2,256,256]{2,1,0:T(8,128)(2,1)}, u32[]{:S(2)}) copy-start(bf16[2,256,256]{2,1,0:T(8,128)(2,1)} %copy-done.9) | copy-start | bytes 786436

commit v3 on v2

--- a/solution.py
+++ b/solution.py
@@ -225,47 +225,53 @@
     return jnp.concatenate([pr.astype(BF16), pi.astype(BF16)], axis=0)
 
 
+class Copies:
+    def __init__(self, sems):
+        self.sems, self.used = sems, 0
+
+    def start(self, source, target, pieces=1):
+        each = source.shape[0] // pieces
+        copies = []
+        for piece in range(pieces):
+            part = pl.ds(piece * each, each)
+            copies.append(pltpu.make_async_copy(source.at[part], target.at[part], self.sems.at[self.used]))
+            copies[-1].start()
+            self.used += 1
+        return copies
+
+
+def finish(copies):
+    for copy in copies:
+        copy.wait()
+
+
+def backward(table, spectrum):
+    return lax.dot_general(table, spectrum, (((0,), (0,)), ((), ())), preferred_element_type=F32)
+
+
 def transforms_kernel(
-    scale,
     fields_hbm,
     taps_hbm,
     forward_hbm,
     back_ref,
-    term_0_ref,
-    term_1_ref,
-    term_2_ref,
-    term_3_ref,
+    cross_ref,
     fields_ref,
     taps_ref,
     forward_ref,
     sections_ref,
     signal_ref,
     spectra_ref,
+    cross_buf,
     parts_ref,
     back_buf,
-    term_buf,
-    load_sems,
-    store_sems,
+    sems,
 ):
-    loads = []
-
-    def load(hbm, vmem, pieces):
-        each = hbm.shape[0] // pieces
-        for piece in range(pieces):
-            part = pl.ds(piece * each, each)
-            loads.append(pltpu.make_async_copy(hbm.at[part], vmem.at[part], load_sems.at[len(loads)]))
-            loads[-1].start()
-        return loads[-pieces:]
-
-    def finish(copies):
-        for copy in copies:
-            copy.wait()
-
+    copies = Copies(sems)
+    first_load = copies.start(fields_hbm.at[:, 0], fields_ref.at[0], 4)
+    second_load = copies.start(fields_hbm.at[:, 1], fields_ref.at[1], 2)
+    forward_load = copies.start(forward_hbm, forward_ref, 2)
+    taps_load = copies.start(taps_hbm, taps_ref, 2)
     stores = []
-
-    def store_copy(source, target):
-        stores.append(pltpu.make_async_copy(source, target, store_sems.at[len(stores)]))
-        stores[-1].start()
 
     def split(i, field):
         split_chunk(
@@ -274,11 +280,7 @@
 
     def gather(i, out):
         def store(n, rows, lanes, y):
-            if out == 2:
-                place = pl.ds(pl.multiple_of((n % 2) * INNER + rows.start, ROWS), ROWS)
-                term_buf[n // 4, (n // 2) % 2, place, lanes] = (y * scale).astype(BF16)
-            else:
-                back_buf[out, n, rows, lanes] = y.astype(BF16)
+            back_buf[out, n, rows, lanes] = y.astype(BF16)
 
         gather_chunk(i, parts_ref.at[out], store)
 
@@ -286,32 +288,22 @@
         return jnp.dot(forward_ref[j], sections_ref[field, j], preferred_element_type=F32)
 
     def inverse(j, out):
-        parts_ref[out, j] = lax.dot_general(
-            forward_ref[j], spectra_ref[out, j], (((0,), (0,)), ((), ())), preferred_element_type=F32
-        )
+        parts_ref[out, j] = backward(forward_ref[j], spectra_ref[out, j])
 
     def multiply(j, lone):
         product, taps, signal = forward(j, 1), taps_ref[j].astype(F32), signal_ref[j]
+        cross_buf[j] = multiply_spectra(signal, product, True, lone)
         spectra_ref[0, j] = multiply_spectra(taps, product, True, lone)
         spectra_ref[1, j] = multiply_spectra(taps, signal, False, lone)
-        spectra_ref[2, j] = multiply_spectra(signal, product, True, lone)
 
     def second_split(i):
         split(i, 1)
         signal_ref[i] = forward(i, 0)
 
     def first_gather(i):
-        gather(i, 2)
-        inverse(i, 0)
-
-    def second_gather(i):
         gather(i, 0)
         inverse(i, 1)
 
-    first_load = load(fields_hbm.at[:, 0], fields_ref.at[0], 4)
-    second_load = load(fields_hbm.at[:, 1], fields_ref.at[1], 2)
-    forward_load = load(forward_hbm, forward_ref, 2)
-    taps_load = load(taps_hbm, taps_ref, 2)
     finish(first_load)
     repeat(lambda i: split(i, 0))
     finish(forward_load + second_load)
@@ -319,48 +311,89 @@
     finish(taps_load)
     for j in range(BLOCKS):
         multiply(j, j == 0)
-    repeat(lambda i: inverse(i, 2))
+        if j > 0:
+            inverse(j - 1, 0)
+    inverse(BLOCKS - 1, 0)
+    stores += copies.start(cross_buf, cross_ref)
     repeat(first_gather)
-    column, side = lax.axis_index("dp") // 2, lax.axis_index("dp") % 2
-    for turn, ref in enumerate((term_0_ref, term_1_ref, term_2_ref, term_3_ref)):
-        for half in range(2):
-            store_copy(term_buf.at[(column + turn) % 4, (side + half) % 2], ref.at[half])
-    repeat(second_gather)
-    store_copy(back_buf.at[0], back_ref.at[:, 0])
+    stores += copies.start(back_buf.at[0], back_ref.at[:, 0])
     for quarter in range(4):
         for i in range(quarter * 4, quarter * 4 + 4):
             gather(i, 1)
         rows = pl.ds(quarter * 2 * ROWS, 2 * ROWS)
-        store_copy(back_buf.at[1, :, rows], back_ref.at[:, 1, rows])
+        stores += copies.start(back_buf.at[1, :, rows], back_ref.at[:, 1, rows])
     finish(stores)
 
 
 def transforms(fields, taps_spec, forward):
     count, _, rows, width = fields.shape
-    length = count * rows
     block = (2 * INNER, width)
     return pl.pallas_call(
-        functools.partial(transforms_kernel, 2.0 / TOTAL / math.sqrt(length)),
+        transforms_kernel,
         in_specs=[HBM] * 3,
-        out_specs=[HBM] * 5,
-        out_shape=[jax.ShapeDtypeStruct(fields.shape, BF16)]
-        + [jax.ShapeDtypeStruct((2, length // 8, width), BF16)] * 4,
+        out_specs=[HBM] * 2,
+        out_shape=[
+            jax.ShapeDtypeStruct(fields.shape, BF16),
+            jax.ShapeDtypeStruct((BLOCKS,) + block, BF16),
+        ],
         scratch_shapes=[
             pltpu.VMEM((2, count, rows, width), BF16),
             pltpu.VMEM((BLOCKS,) + block, BF16),
             pltpu.VMEM(forward.shape, BF16),
             pltpu.VMEM((2, BLOCKS) + block, BF16),
             pltpu.VMEM((BLOCKS,) + block, F32),
-            pltpu.VMEM((3, BLOCKS) + block, BF16),
-            pltpu.VMEM((3, BLOCKS) + block, F32),
+            pltpu.VMEM((2, BLOCKS) + block, BF16),
+            pltpu.VMEM((BLOCKS,) + block, BF16),
+            pltpu.VMEM((2, BLOCKS) + block, F32),
             pltpu.VMEM((2, count, rows, width), BF16),
-            pltpu.VMEM((4, 2, length // 8, width), BF16),
             pltpu.SemaphoreType.DMA((16,)),
-            pltpu.SemaphoreType.DMA((13,)),
         ],
         compiler_params=pltpu.CompilerParams(vmem_limit_bytes=61 << 20),
         name="transforms",
     )(fields, taps_spec, forward)
+
+
+def term_kernel(scale, cross_hbm, forward_hbm, *refs):
+    targets = refs[:8]
+    cross_ref, forward_ref, parts_ref, term_buf, sems = refs[8:]
+    copies = Copies(sems)
+    loads = copies.start(forward_hbm, forward_ref, 2) + copies.start(cross_hbm, cross_ref, 2)
+
+    def store(n, rows, lanes, y):
+        place = pl.ds(pl.multiple_of((n % 2) * INNER + rows.start, ROWS), ROWS)
+        term_buf[n // 4, (n // 2) % 2, place, lanes] = (y * scale).astype(BF16)
+
+    finish(loads)
+    for j in range(BLOCKS):
+        parts_ref[j] = backward(forward_ref[j], cross_ref[j])
+    repeat(lambda i: gather_chunk(i, parts_ref, store))
+    column, side = lax.axis_index("dp") // 2, lax.axis_index("dp") % 2
+    stores = []
+    for half in (1, 0):
+        for turn in range(4):
+            ref = targets[4 * half + turn]
+            stores += copies.start(term_buf.at[(column + turn) % 4, (side + half) % 2], ref)
+    finish(stores)
+
+
+def filter_term(cross, forward, length):
+    share = (length // 8, cross.shape[2])
+    refs = pl.pallas_call(
+        functools.partial(term_kernel, 2.0 / TOTAL / math.sqrt(length)),
+        in_specs=[HBM] * 2,
+        out_specs=[HBM] * 8,
+        out_shape=[jax.ShapeDtypeStruct(share, BF16)] * 8,
+        scratch_shapes=[
+            pltpu.VMEM(cross.shape, BF16),
+            pltpu.VMEM(forward.shape, BF16),
+            pltpu.VMEM(cross.shape, F32),
+            pltpu.VMEM((4, 2) + share, BF16),
+            pltpu.SemaphoreType.DMA((12,)),
+        ],
+        compiler_params=pltpu.CompilerParams(vmem_limit_bytes=61 << 20),
+        name="filter_term",
+    )(cross, forward)
+    return refs[:4], refs[4:]
 
 
 def outputs_kernel(back_ref, cotangent_ref, signal_grad_ref, gate_grad_ref, gate_buf, sems):
@@ -397,13 +430,18 @@
     )(back, cotangent)
 
 
-def sum_over_sequences(quarters):
+def sum_over_sequences(own, others):
     devices = lax.axis_size("dp")
-    terms = [quarters[0]]
-    for turn in (2, 1, 3):
-        terms.append(lax.ppermute(quarters[turn], "dp", [(d, (d + 2 * turn) % devices) for d in range(devices)]))
-    keep, away = (sum(term[half].astype(F32) for term in terms) for half in range(2))
-    return keep, lax.ppermute(away.astype(BF16), "dp", [(d, d ^ 1) for d in range(devices)])
+
+    def round_y(terms):
+        moved = [terms[0]]
+        for turn in (2, 1, 3):
+            moved.append(lax.ppermute(terms[turn], "dp", [(d, (d + 2 * turn) % devices) for d in range(devices)]))
+        return sum(term.astype(F32) for term in moved)
+
+    away = round_y(others).astype(BF16)
+    other = lax.ppermute(away, "dp", [(d, d ^ 1) for d in range(devices)])
+    return round_y(own), other
 
 
 def local(signal, gate, cotangent, filter_taps):
@@ -411,9 +449,9 @@
     forward = section_tables()
     fields = lax.all_to_all(send_fields(signal, gate, cotangent, count), "ctx", 0, 0, tiled=True)
     taps_spec = taps_spectrum(filter_taps, forward)
-    back, *quarters = transforms(fields, taps_spec, forward)
+    back, cross = transforms(fields, taps_spec, forward)
     back = lax.all_to_all(back, "ctx", 0, 0, tiled=True)
-    keep, other = sum_over_sequences(quarters)
+    keep, other = sum_over_sequences(*filter_term(cross, forward, filter_taps.shape[0]))
     signal_grad, gate_grad = place_outputs(back, cotangent)
     signal_grad, other = lax.optimization_barrier((signal_grad, other))
     return (signal_grad, gate_grad, keep + other.astype(F32))

time: 90.5 us -> 88.4 us (0.977)
  the two profiles are of different devices: /device:TPU:40 before, /device:TPU:0 now
where the time goes in v3:
time: 88.4 us; the launch traced here: 86.7 us
  waiting for transfers between devices  32.5 us (37%)
  starting transfers between devices  26.8 us (30%)
  Pallas kernels  20.8 us (24%)
  local copies, waits for them, and re-layouts  4.18 us (5%)
  other arithmetic  1.76 us (2%)
    all_to_all x1, waiting for transfers between devices, local(): lax.all_to_all(send_fields(signal, gate, cotangent, count), 'ctx', 0, 0,...  23.8 us
    ppermute x6, starting transfers between devices, round_y(): lax.ppermute(terms[turn], 'dp', [(d, (d + 2 * turn) % devices) for d in r...  11.8 us
    pallas_call x1, Pallas kernels, transforms(): pl.pallas_call(transforms_kernel, in_specs=[HBM] * 3, out_specs=[HBM] * 2...  9.41 us
    all_to_all x1, starting transfers between devices, local(): lax.all_to_all(send_fields(signal, gate, cotangent, count), 'ctx', 0, 0,...  6.62 us
    all_to_all x1, starting transfers between devices, local(): back = lax.all_to_all(back, 'ctx', 0, 0, tiled=True)  5.54 us
    pallas_call x1, Pallas kernels, filter_term(): pl.pallas_call(functools.partial(term_kernel, 2.0 / TOTAL / math.sqrt(len...  4.95 us
    all_to_all x1, waiting for transfers between devices, local(): back = lax.all_to_all(back, 'ctx', 0, 0, tiled=True)  4.39 us
    ppermute x6, waiting for transfers between devices, round_y(): lax.ppermute(terms[turn], 'dp', [(d, (d + 2 * turn) % devices) for d in r...  4.27 us
  transfers between devices with their start and end apart: 9, of which 5 were waited for; matrix products, arithmetic and copies ran while one was open for 1% of the time, Pallas kernels for 10%

profile of v3, /device:TPU:0, one launch (start us, length us, event | category | flops | bytes accessed | tf_op | source)
XLA Modules:
  0.0 86.7 jit_solution(9816399433456684838)
XLA Ops:
  0.6 2.9 %product.1 = bf16[16,2,128,256]{3,2,1,0:T(8,128)(2,1)} custom-call(bf16[1,128,4096]{2,1,0:T(8,128)(2,1)} %signal_ref.1, bf16[1,128,4096]{2,1,0:T(8,128)(2,1)} %gate_ref.1, bf16[1,128,4096]{2,1,0:T(8,128)(2,1)} %cotangent_ref.3), custom_call_target="tpu_custom_call" | custom-call | tf_op jit(solution)/shard_map/product/pallas_call | solution.py:149
  3.5 6.6 %all-to-all-start = ((bf16[16,2,128,256]{3,2,1,0:T(8,128)(2,1)}), bf16[16,2,128,256]{3,2,1,0:T(8,128)(2,1)}, u32[]{:S(2)}, u32[]{:S(2)}) async-start(bf16[16,2,128,256]{3,2,1,0:T(8,128)(2,1)} %product.1), calls=%async_computation | async-start | bytes 4194304 | tf_op jit(solution)/shard_map/all_to_all | solution.py:450
  10.2 1.6 %copy-done.3 = f32[2048,256]{1,0:T(8,128)S(1)} copy-done((f32[2048,256]{1,0:T(8,128)S(1)}, f32[2048,256]{1,0:T(8,128)}, u32[]{:S(2)}) %copy-start.3) | copy-done | bytes 2097176
  11.8 2.1 %taps_spectrum.1.taps_hbm = bf16[16,256,256]{2,1,0:T(8,128)(2,1)S(1)} custom-call(f32[2048,256]{1,0:T(8,128)S(1)} %copy-done.3, bf16[16,256,256]{2,1,0:T(8,128)(2,1)S(1)} %copy-done), custom_call_target="tpu_custom_call" | custom-call | tf_op jit(solution)/shard_map/taps_spectrum/pallas_call | solution.py:205
  13.9 1.4 %copy-done.1 = bf16[16,256,256]{2,1,0:T(8,128)(2,1)} copy-done((bf16[16,256,256]{2,1,0:T(8,128)(2,1)}, bf16[16,256,256]{2,1,0:T(8,128)(2,1)S(1)}, u32[]{:S(2)}) %copy-start.1) | copy-done | bytes 2097176
  15.2 23.8 %all-to-all-done.fields_hbm = bf16[16,2,128,256]{3,2,1,0:T(8,128)(2,1)} async-done(((bf16[16,2,128,256]{3,2,1,0:T(8,128)(2,1)}), bf16[16,2,128,256]{3,2,1,0:T(8,128)(2,1)}, u32[]{:S(2)}, u32[]{:S(2)}) %all-to-all-start) | async-done | bytes 2097184 | tf_op jit(solution)/shard_map/all_to_all | solution.py:450
  39.0 9.4 %transforms.1 = (bf16[16,2,128,256]{3,2,1,0:T(8,128)(2,1)}, bf16[16,256,256]{2,1,0:T(8,128)(2,1)}) custom-call(bf16[16,2,128,256]{3,2,1,0:T(8,128)(2,1)} %all-to-all-done.fields_hbm, bf16[16,256,256]{2,1,0:T(8,128)(2,1)} %copy-done.1, bf16[16,256,256]{2,1,0:T(8,128)(2,1)} %constant.2.clone.forward_ref.forward_hbm), custom_call_target="tpu_custom_call" | custom-call | tf_op jit(solution)/shard_map/transforms/pallas_call | solution.py:331
  48.4 5.5 %all-to-all-start.1 = ((bf16[16,2,128,256]{3,2,1,0:T(8,128)(2,1)}), bf16[16,2,128,256]{3,2,1,0:T(8,128)(2,1)S(1)}, u32[]{:S(2)}, u32[]{:S(2)}) async-start(bf16[16,2,128,256]{3,2,1,0:T(8,128)(2,1)} %get-tuple-element.17), calls=%async_computation.1 | async-start | bytes 4194304 | tf_op jit(solution)/shard_map/all_to_all | solution.py:453
  54.0 5.0 %filter_term.1 = (bf16[256,256]{1,0:T(8,128)(2,1)}, bf16[256,256]{1,0:T(8,128)(2,1)}, bf16[256,256]{1,0:T(8,128)(2,1)}, bf16[256,256]{1,0:T(8,128)(2,1)}, bf16[2...) custom-call(bf16[16,256,256]{2,1,0:T(8,128)(2,1)} %get-tuple-element.19.cros, ...), custom_call_target="tpu_custom_call" | custom-call | tf_op jit(solution)/shard_map/filter_term/pallas_call | solution.py:381
  58.9 3.3 %collective-permute-start = (bf16[256,256]{1,0:T(8,128)(2,1)}, bf16[256,256]{1,0:T(8,128)(2,1)S(1)}, u32[]{:S(2)}, u32[]{:S(2)}) collective-permute-start(bf16[256,256]{1,0:T(8,128)(2,1)} %get-tuple-element.21), channel_id=1, source_target_pairs={{0,64},{16,80},{32,96},{48,112},{64,0},{80,16},{96,32},{112,48},{1... | collective-permute-start | bytes 393224 | tf_op jit(solution)/shard_map/ppermute | solution.py:439
  62.2 0.7 collective-permute-start.1
  62.9 2.6 %collective-permute-start.2 = (bf16[256,256]{1,0:T(8,128)(2,1)}, bf16[256,256]{1,0:T(8,128)(2,1)S(1)}, u32[]{:S(2)}, u32[]{:S(2)}) collective-permute-start(bf16[256,256]{1,0:T(8,128)(2,1)} %get-tuple-element.23), channel_id=1, source_target_pairs={{0,96},{16,112},{32,0},{48,16},{64,32},{80,48},{96,64},{112,80},{1... | collective-permute-start | bytes 393224 | tf_op jit(solution)/shard_map/ppermute | solution.py:439
  65.4 1.6 %collective-permute-done = bf16[256,256]{1,0:T(8,128)(2,1)S(1)} collective-permute-done((bf16[256,256]{1,0:T(8,128)(2,1)}, bf16[256,256]{1,0:T(8,128)(2,1)S(1)}, u32[]{:S(2)}, u32[]{:S(2)}) %collective-permute-start) | collective-permute-done | bytes 131104 | tf_op jit(solution)/shard_map/ppermute | solution.py:439
  67.0 2.5 %collective-permute-done.1 = bf16[256,256]{1,0:T(8,128)(2,1)S(1)} collective-permute-done((bf16[256,256]{1,0:T(8,128)(2,1)}, bf16[256,256]{1,0:T(8,128)(2,1)S(1)}, u32[]{:S(2)}, u32[]{:S(2)}) %collective-permute-start.1) | collective-permute-done | bytes 131104 | tf_op jit(solution)/shard_map/ppermute | solution.py:439
  69.5 0.2 collective-permute-done.2
  69.7 1.0 %add_convert_fusion = bf16[256,256]{1,0:T(8,128)(2,1)S(1)} fusion(bf16[256,256]{1,0:T(8,128)(2,1)S(1)} %collective-permute-done.2, bf16[256,256]{1,0:T(8,128)(2,1)S(1)} %collective-permute-done.1, bf16[256,256]{1,0:T(8,128)(2,1)S(1)} %collective-permute-done, bf16[256,256]{1,0:T(8,128)(2,1)} %get-tuple-element.20), kind=kLoop, calls=%fused_computation.1 | loop fusion | flops 524288 | bytes 655360 | tf_op jit(solution)/shard_map/convert_element_type | solution.py:442
  70.7 2.8 %collective-permute-start.3 = (bf16[256,256]{1,0:T(8,128)(2,1)S(1)}, bf16[256,256]{1,0:T(8,128)(2,1)S(1)}, u32[]{:S(2)}, u32[]{:S(2)}) collective-permute-start(bf16[256,256]{1,0:T(8,128)(2,1)S(1)} %add_convert_fusion), channel_id=1, source_target_pairs={{0,16},{16,0},{32,48},{48,32},{64,80},{80,64},{96,112},{112,96},{1... | collective-permute-start | bytes 393224 | tf_op jit(solution)/shard_map/ppermute | solution.py:443
  73.5 2.1 %collective-permute-start.4 = (bf16[256,256]{1,0:T(8,128)(2,1)}, bf16[256,256]{1,0:T(8,128)(2,1)S(1)}, u32[]{:S(2)}, u32[]{:S(2)}) collective-permute-start(bf16[256,256]{1,0:T(8,128)(2,1)} %get-tuple-element.27), channel_id=1, source_target_pairs={{0,64},{16,80},{32,96},{48,112},{64,0},{80,16},{96,32},{112,48},{1... | collective-permute-start | bytes 393224 | tf_op jit(solution)/shard_map/ppermute | solution.py:439
  75.6 1.6 %collective-permute-start.5 = (bf16[256,256]{1,0:T(8,128)(2,1)}, bf16[256,256]{1,0:T(8,128)(2,1)S(1)}, u32[]{:S(2)}, u32[]{:S(2)}) collective-permute-start(bf16[256,256]{1,0:T(8,128)(2,1)} %get-tuple-element.28), channel_id=1, source_target_pairs={{0,32},{16,48},{32,64},{48,80},{64,96},{80,112},{96,0},{112,16},{1... | collective-permute-start | bytes 393224 | tf_op jit(solution)/shard_map/ppermute | solution.py:439
  77.1 1.7 %collective-permute-start.6 = (bf16[256,256]{1,0:T(8,128)(2,1)}, bf16[256,256]{1,0:T(8,128)(2,1)S(1)}, u32[]{:S(2)}, u32[]{:S(2)}) collective-permute-start(bf16[256,256]{1,0:T(8,128)(2,1)} %get-tuple-element.29), channel_id=1, source_target_pairs={{0,96},{16,112},{32,0},{48,16},{64,32},{80,48},{96,64},{112,80},{1... | collective-permute-start | bytes 393224 | tf_op jit(solution)/shard_map/ppermute | solution.py:439
  78.8 4.4 %all-to-all-done.1.back_ref = bf16[16,2,128,256]{3,2,1,0:T(8,128)(2,1)S(1)} async-done(((bf16[16,2,128,256]{3,2,1,0:T(8,128)(2,1)}), bf16[16,2,128,256]{3,2,1,0:T(8,128)(2,1)S(1)}, u32[]{:S(2)}, u32[]{:S(2)}) %all-to-all-start.1) | async-done | bytes 2097184 | tf_op jit(solution)/shard_map/all_to_all | solution.py:453
  83.2 1.2 %copy-done.2 = bf16[1,128,4096]{2,1,0:T(8,128)(2,1)S(1)} copy-done((bf16[1,128,4096]{2,1,0:T(8,128)(2,1)S(1)}, bf16[1,128,4096]{2,1,0:T(8,128)(2,1)}, u32[]{:S(2)}) %copy-start.2) | copy-done | bytes 1048600
  84.4 1.5 %outputs.1 = (bf16[1,128,4096]{2,1,0:T(8,128)(2,1)}, bf16[1,128,4096]{2,1,0:T(8,128)(2,1)}) custom-call(bf16[16,2,128,256]{3,2,1,0:T(8,128)(2,1)S(1)} %all-to-all-done.1.back_ref, bf16[1,128,4096]{2,1,0:T(8,128)(2,1)S(1)} %copy-done.2), custom_call_target="tpu_custom_call" | custom-call | tf_op jit(solution)/shard_map/outputs/pallas_call | solution.py:419
  86.0 0.8 convert_add_fusion
  (11 shorter events, 0.0 us)
Async XLA Ops:
  3.5 6.6 %copy-start = (bf16[16,256,256]{2,1,0:T(8,128)(2,1)S(1)}, bf16[16,256,256]{2,1,0:T(8,128)(2,1)}, u32[]{:S(2)}) copy-start(bf16[16,256,256]{2,1,0:T(8,128)(2,1)} %constant.2.clone.forward_ref.forward_hbm) | copy-start | bytes 6291460
  3.5 35.4 %all-to-all-start = ((bf16[16,2,128,256]{3,2,1,0:T(8,128)(2,1)}), bf16[16,2,128,256]{3,2,1,0:T(8,128)(2,1)}, u32[]{:S(2)}, u32[]{:S(2)}) async-start(bf16[16,2,128,256]{3,2,1,0:T(8,128)(2,1)} %product.1), calls=%async_computation | async-start | bytes 4194304 | tf_op jit(solution)/shard_map/all_to_all | solution.py:450
  10.2 1.6 %copy-start.3 = (f32[2048,256]{1,0:T(8,128)S(1)}, f32[2048,256]{1,0:T(8,128)}, u32[]{:S(2)}) copy-start(f32[2048,256]{1,0:T(8,128)} %taps_ref.1) | copy-start | bytes 6291460
  13.8 1.4 %copy-start.1 = (bf16[16,256,256]{2,1,0:T(8,128)(2,1)}, bf16[16,256,256]{2,1,0:T(8,128)(2,1)S(1)}, u32[]{:S(2)}) copy-start(bf16[16,256,256]{2,1,0:T(8,128)(2,1)S(1)} %taps_spectrum.1.taps_hbm) | copy-start | bytes 6291460
  48.4 34.8 %all-to-all-start.1 = ((bf16[16,2,128,256]{3,2,1,0:T(8,128)(2,1)}), bf16[16,2,128,256]{3,2,1,0:T(8,128)(2,1)S(1)}, u32[]{:S(2)}, u32[]{:S(2)}) async-start(bf16[16,2,128,256]{3,2,1,0:T(8,128)(2,1)} %get-tuple-element.17), calls=%async_computation.1 | async-start | bytes 4194304 | tf_op jit(solution)/shard_map/all_to_all | solution.py:453
  58.9 27.0 %copy-start.4 = (bf16[256,256]{1,0:T(8,128)(2,1)S(1)}, bf16[256,256]{1,0:T(8,128)(2,1)}, u32[]{:S(2)}) copy-start(bf16[256,256]{1,0:T(8,128)(2,1)} %get-tuple-element.26) | copy-start | bytes 393220
  58.9 8.1 %collective-permute-start = (bf16[256,256]{1,0:T(8,128)(2,1)}, bf16[256,256]{1,0:T(8,128)(2,1)S(1)}, u32[]{:S(2)}, u32[]{:S(2)}) collective-permute-start(bf16[256,256]{1,0:T(8,128)(2,1)} %get-tuple-element.21), channel_id=1, source_target_pairs={{0,64},{16,80},{32,96},{48,112},{64,0},{80,16},{96,32},{112,48},{1... | collective-permute-start | bytes 393224 | tf_op jit(solution)/shard_map/ppermute | solution.py:439
  62.2 7.3 %collective-permute-start.1 = (bf16[256,256]{1,0:T(8,128)(2,1)}, bf16[256,256]{1,0:T(8,128)(2,1)S(1)}, u32[]{:S(2)}, u32[]{:S(2)}) collective-permute-start(bf16[256,256]{1,0:T(8,128)(2,1)} %get-tuple-element.22), channel_id=1, source_target_pairs={{0,32},{16,48},{32,64},{48,80},{64,96},{80,112},{96,0},{112,16},{1... | collective-permute-start | bytes 393224 | tf_op jit(solution)/shard_map/ppermute | solution.py:439
  62.9 6.8 %collective-permute-start.2 = (bf16[256,256]{1,0:T(8,128)(2,1)}, bf16[256,256]{1,0:T(8,128)(2,1)S(1)}, u32[]{:S(2)}, u32[]{:S(2)}) collective-permute-start(bf16[256,256]{1,0:T(8,128)(2,1)} %get-tuple-element.23), channel_id=1, source_target_pairs={{0,96},{16,112},{32,0},{48,16},{64,32},{80,48},{96,64},{112,80},{1... | collective-permute-start | bytes 393224 | tf_op jit(solution)/shard_map/ppermute | solution.py:439
  70.7 15.2 %collective-permute-start.3 = (bf16[256,256]{1,0:T(8,128)(2,1)S(1)}, bf16[256,256]{1,0:T(8,128)(2,1)S(1)}, u32[]{:S(2)}, u32[]{:S(2)}) collective-permute-start(bf16[256,256]{1,0:T(8,128)(2,1)S(1)} %add_convert_fusion), channel_id=1, source_target_pairs={{0,16},{16,0},{32,48},{48,32},{64,80},{80,64},{96,112},{112,96},{1... | collective-permute-start | bytes 393224 | tf_op jit(solution)/shard_map/ppermute | solution.py:443
  73.5 12.4 %collective-permute-start.4 = (bf16[256,256]{1,0:T(8,128)(2,1)}, bf16[256,256]{1,0:T(8,128)(2,1)S(1)}, u32[]{:S(2)}, u32[]{:S(2)}) collective-permute-start(bf16[256,256]{1,0:T(8,128)(2,1)} %get-tuple-element.27), channel_id=1, source_target_pairs={{0,64},{16,80},{32,96},{48,112},{64,0},{80,16},{96,32},{112,48},{1... | collective-permute-start | bytes 393224 | tf_op jit(solution)/shard_map/ppermute | solution.py:439
  75.6 10.4 %collective-permute-start.5 = (bf16[256,256]{1,0:T(8,128)(2,1)}, bf16[256,256]{1,0:T(8,128)(2,1)S(1)}, u32[]{:S(2)}, u32[]{:S(2)}) collective-permute-start(bf16[256,256]{1,0:T(8,128)(2,1)} %get-tuple-element.28), channel_id=1, source_target_pairs={{0,32},{16,48},{32,64},{48,80},{64,96},{80,112},{96,0},{112,16},{1... | collective-permute-start | bytes 393224 | tf_op jit(solution)/shard_map/ppermute | solution.py:439
  77.1 8.8 %collective-permute-start.6 = (bf16[256,256]{1,0:T(8,128)(2,1)}, bf16[256,256]{1,0:T(8,128)(2,1)S(1)}, u32[]{:S(2)}, u32[]{:S(2)}) collective-permute-start(bf16[256,256]{1,0:T(8,128)(2,1)} %get-tuple-element.29), channel_id=1, source_target_pairs={{0,96},{16,112},{32,0},{48,16},{64,32},{80,48},{96,64},{112,80},{1... | collective-permute-start | bytes 393224 | tf_op jit(solution)/shard_map/ppermute | solution.py:439
  83.2 1.2 %copy-start.2 = (bf16[1,128,4096]{2,1,0:T(8,128)(2,1)S(1)}, bf16[1,128,4096]{2,1,0:T(8,128)(2,1)}, u32[]{:S(2)}) copy-start(bf16[1,128,4096]{2,1,0:T(8,128)(2,1)} %cotangent_ref.3) | copy-start | bytes 3145732

commit v4 on v3

--- a/solution.py
+++ b/solution.py
@@ -267,7 +267,10 @@
     sems,
 ):
     copies = Copies(sems)
-    first_load = copies.start(fields_hbm.at[:, 0], fields_ref.at[0], 4)
+    first_load = []
+    for part in range(PARTS):
+        rows = pl.ds(part * (INNER // PARTS), INNER // PARTS)
+        first_load += copies.start(fields_hbm.at[:, 0, rows], fields_ref.at[0, :, rows])
     second_load = copies.start(fields_hbm.at[:, 1], fields_ref.at[1], 2)
     forward_load = copies.start(forward_hbm, forward_ref, 2)
     taps_load = copies.start(taps_hbm, taps_ref, 2)
@@ -304,8 +307,10 @@
         gather(i, 0)
         inverse(i, 1)
 
-    finish(first_load)
-    repeat(lambda i: split(i, 0))
+    for i in range(BLOCKS):
+        if i % (BLOCKS // PARTS) == 0:
+            first_load[i // (BLOCKS // PARTS)].wait()
+        split(i, 0)
     finish(forward_load + second_load)
     repeat(second_split)
     finish(taps_load)
@@ -357,14 +362,21 @@
     targets = refs[:8]
     cross_ref, forward_ref, parts_ref, term_buf, sems = refs[8:]
     copies = Copies(sems)
-    loads = copies.start(forward_hbm, forward_ref, 2) + copies.start(cross_hbm, cross_ref, 2)
+    loads = []
+    for part in range(PARTS):
+        blocks = pl.ds(part * (BLOCKS // PARTS), BLOCKS // PARTS)
+        loads.append(
+            copies.start(forward_hbm.at[blocks], forward_ref.at[blocks])
+            + copies.start(cross_hbm.at[blocks], cross_ref.at[blocks])
+        )
 
     def store(n, rows, lanes, y):
         place = pl.ds(pl.multiple_of((n % 2) * INNER + rows.start, ROWS), ROWS)
         term_buf[n // 4, (n // 2) % 2, place, lanes] = (y * scale).astype(BF16)
 
-    finish(loads)
     for j in range(BLOCKS):
+        if j % (BLOCKS // PARTS) == 0:
+            finish(loads[j // (BLOCKS // PARTS)])
         parts_ref[j] = backward(forward_ref[j], cross_ref[j])
     repeat(lambda i: gather_chunk(i, parts_ref, store))
     column, side = lax.axis_index("dp") // 2, lax.axis_index("dp") % 2
@@ -388,7 +400,7 @@
             pltpu.VMEM(forward.shape, BF16),
             pltpu.VMEM(cross.shape, F32),
             pltpu.VMEM((4, 2) + share, BF16),
-            pltpu.SemaphoreType.DMA((12,)),
+            pltpu.SemaphoreType.DMA((8 + 2 * PARTS,)),
         ],
         compiler_params=pltpu.CompilerParams(vmem_limit_bytes=61 << 20),
         name="filter_term",

time: 88.4 us -> 88.3 us (level)
  no operation moved by 1% of the time
where the time goes in v4:
time: 88.3 us; the launch traced here: 86.6 us
  waiting for transfers between devices  32.7 us (37%)
  starting transfers between devices  26.8 us (30%)
  Pallas kernels  20.4 us (23%)
  local copies, waits for them, and re-layouts  4.18 us (5%)
  other arithmetic  1.76 us (2%)
    all_to_all x1, waiting for transfers between devices, local(): lax.all_to_all(send_fields(signal, gate, cotangent, count), 'ctx', 0, 0,...  23.8 us
    ppermute x6, starting transfers between devices, round_y(): lax.ppermute(terms[turn], 'dp', [(d, (d + 2 * turn) % devices) for d in r...  11.8 us
    pallas_call x1, Pallas kernels, transforms(): pl.pallas_call(transforms_kernel, in_specs=[HBM] * 3, out_specs=[HBM] * 2...  9.32 us
    all_to_all x1, starting transfers between devices, local(): lax.all_to_all(send_fields(signal, gate, cotangent, count), 'ctx', 0, 0,...  6.62 us
    all_to_all x1, starting transfers between devices, local(): back = lax.all_to_all(back, 'ctx', 0, 0, tiled=True)  5.53 us
    pallas_call x1, Pallas kernels, filter_term(): pl.pallas_call(functools.partial(term_kernel, 2.0 / TOTAL / math.sqrt(len...  4.7 us
    all_to_all x1, waiting for transfers between devices, local(): back = lax.all_to_all(back, 'ctx', 0, 0, tiled=True)  4.63 us
    ppermute x6, waiting for transfers between devices, round_y(): lax.ppermute(terms[turn], 'dp', [(d, (d + 2 * turn) % devices) for d in r...  4.27 us
  transfers between devices with their start and end apart: 9, of which 5 were waited for; matrix products, arithmetic and copies ran while one was open for 1% of the time, Pallas kernels for 10%

profile of v4, /device:TPU:0, one launch (start us, length us, event | category | flops | bytes accessed | tf_op | source)
XLA Modules:
  0.0 86.6 jit_solution(9947422619393463915)
XLA Ops:
  0.6 2.9 %product.1 = bf16[16,2,128,256]{3,2,1,0:T(8,128)(2,1)} custom-call(bf16[1,128,4096]{2,1,0:T(8,128)(2,1)} %signal_ref.1, bf16[1,128,4096]{2,1,0:T(8,128)(2,1)} %gate_ref.1, bf16[1,128,4096]{2,1,0:T(8,128)(2,1)} %cotangent_ref.3), custom_call_target="tpu_custom_call" | custom-call | tf_op jit(solution)/shard_map/product/pallas_call | solution.py:149
  3.5 6.6 %all-to-all-start = ((bf16[16,2,128,256]{3,2,1,0:T(8,128)(2,1)}), bf16[16,2,128,256]{3,2,1,0:T(8,128)(2,1)}, u32[]{:S(2)}, u32[]{:S(2)}) async-start(bf16[16,2,128,256]{3,2,1,0:T(8,128)(2,1)} %product.1), calls=%async_computation | async-start | bytes 4194304 | tf_op jit(solution)/shard_map/all_to_all | solution.py:462
  10.2 1.6 %copy-done.3 = f32[2048,256]{1,0:T(8,128)S(1)} copy-done((f32[2048,256]{1,0:T(8,128)S(1)}, f32[2048,256]{1,0:T(8,128)}, u32[]{:S(2)}) %copy-start.3) | copy-done | bytes 2097176
  11.8 2.1 %taps_spectrum.1.taps_hbm = bf16[16,256,256]{2,1,0:T(8,128)(2,1)S(1)} custom-call(f32[2048,256]{1,0:T(8,128)S(1)} %copy-done.3, bf16[16,256,256]{2,1,0:T(8,128)(2,1)S(1)} %copy-done), custom_call_target="tpu_custom_call" | custom-call | tf_op jit(solution)/shard_map/taps_spectrum/pallas_call | solution.py:205
  13.9 1.4 %copy-done.1 = bf16[16,256,256]{2,1,0:T(8,128)(2,1)} copy-done((bf16[16,256,256]{2,1,0:T(8,128)(2,1)}, bf16[16,256,256]{2,1,0:T(8,128)(2,1)S(1)}, u32[]{:S(2)}) %copy-start.1) | copy-done | bytes 2097176
  15.2 23.8 %all-to-all-done.fields_hbm = bf16[16,2,128,256]{3,2,1,0:T(8,128)(2,1)} async-done(((bf16[16,2,128,256]{3,2,1,0:T(8,128)(2,1)}), bf16[16,2,128,256]{3,2,1,0:T(8,128)(2,1)}, u32[]{:S(2)}, u32[]{:S(2)}) %all-to-all-start) | async-done | bytes 2097184 | tf_op jit(solution)/shard_map/all_to_all | solution.py:462
  39.0 9.3 %transforms.1 = (bf16[16,2,128,256]{3,2,1,0:T(8,128)(2,1)}, bf16[16,256,256]{2,1,0:T(8,128)(2,1)}) custom-call(bf16[16,2,128,256]{3,2,1,0:T(8,128)(2,1)} %all-to-all-done.fields_hbm, bf16[16,256,256]{2,1,0:T(8,128)(2,1)} %copy-done.1, bf16[16,256,256]{2,1,0:T(8,128)(2,1)} %constant.2.clone.forward_ref.forward_hbm), custom_call_target="tpu_custom_call" | custom-call | tf_op jit(solution)/shard_map/transforms/pallas_call | solution.py:336
  48.3 5.5 %all-to-all-start.1 = ((bf16[16,2,128,256]{3,2,1,0:T(8,128)(2,1)}), bf16[16,2,128,256]{3,2,1,0:T(8,128)(2,1)S(1)}, u32[]{:S(2)}, u32[]{:S(2)}) async-start(bf16[16,2,128,256]{3,2,1,0:T(8,128)(2,1)} %get-tuple-element.17), calls=%async_computation.1 | async-start | bytes 4194304 | tf_op jit(solution)/shard_map/all_to_all | solution.py:465
  53.9 4.7 %filter_term.1 = (bf16[256,256]{1,0:T(8,128)(2,1)}, bf16[256,256]{1,0:T(8,128)(2,1)}, bf16[256,256]{1,0:T(8,128)(2,1)}, bf16[256,256]{1,0:T(8,128)(2,1)}, bf16[2...) custom-call(bf16[16,256,256]{2,1,0:T(8,128)(2,1)} %get-tuple-element.19.cros, ...), custom_call_target="tpu_custom_call" | custom-call | tf_op jit(solution)/shard_map/filter_term/pallas_call | solution.py:393
  58.6 3.3 %collective-permute-start = (bf16[256,256]{1,0:T(8,128)(2,1)}, bf16[256,256]{1,0:T(8,128)(2,1)S(1)}, u32[]{:S(2)}, u32[]{:S(2)}) collective-permute-start(bf16[256,256]{1,0:T(8,128)(2,1)} %get-tuple-element.21), channel_id=1, source_target_pairs={{0,64},{16,80},{32,96},{48,112},{64,0},{80,16},{96,32},{112,48},{1... | collective-permute-start | bytes 393224 | tf_op jit(solution)/shard_map/ppermute | solution.py:451
  61.8 0.7 collective-permute-start.1
  62.5 2.6 %collective-permute-start.2 = (bf16[256,256]{1,0:T(8,128)(2,1)}, bf16[256,256]{1,0:T(8,128)(2,1)S(1)}, u32[]{:S(2)}, u32[]{:S(2)}) collective-permute-start(bf16[256,256]{1,0:T(8,128)(2,1)} %get-tuple-element.23), channel_id=1, source_target_pairs={{0,96},{16,112},{32,0},{48,16},{64,32},{80,48},{96,64},{112,80},{1... | collective-permute-start | bytes 393224 | tf_op jit(solution)/shard_map/ppermute | solution.py:451
  65.1 1.6 %collective-permute-done = bf16[256,256]{1,0:T(8,128)(2,1)S(1)} collective-permute-done((bf16[256,256]{1,0:T(8,128)(2,1)}, bf16[256,256]{1,0:T(8,128)(2,1)S(1)}, u32[]{:S(2)}, u32[]{:S(2)}) %collective-permute-start) | collective-permute-done | bytes 131104 | tf_op jit(solution)/shard_map/ppermute | solution.py:451
  66.7 2.5 %collective-permute-done.1 = bf16[256,256]{1,0:T(8,128)(2,1)S(1)} collective-permute-done((bf16[256,256]{1,0:T(8,128)(2,1)}, bf16[256,256]{1,0:T(8,128)(2,1)S(1)}, u32[]{:S(2)}, u32[]{:S(2)}) %collective-permute-start.1) | collective-permute-done | bytes 131104 | tf_op jit(solution)/shard_map/ppermute | solution.py:451
  69.2 0.2 collective-permute-done.2
  69.4 1.0 %add_convert_fusion = bf16[256,256]{1,0:T(8,128)(2,1)S(1)} fusion(bf16[256,256]{1,0:T(8,128)(2,1)S(1)} %collective-permute-done.2, bf16[256,256]{1,0:T(8,128)(2,1)S(1)} %collective-permute-done.1, bf16[256,256]{1,0:T(8,128)(2,1)S(1)} %collective-permute-done, bf16[256,256]{1,0:T(8,128)(2,1)} %get-tuple-element.20), kind=kLoop, calls=%fused_computation.1 | loop fusion | flops 524288 | bytes 655360 | tf_op jit(solution)/shard_map/convert_element_type | solution.py:454
  70.3 2.8 %collective-permute-start.3 = (bf16[256,256]{1,0:T(8,128)(2,1)S(1)}, bf16[256,256]{1,0:T(8,128)(2,1)S(1)}, u32[]{:S(2)}, u32[]{:S(2)}) collective-permute-start(bf16[256,256]{1,0:T(8,128)(2,1)S(1)} %add_convert_fusion), channel_id=1, source_target_pairs={{0,16},{16,0},{32,48},{48,32},{64,80},{80,64},{96,112},{112,96},{1... | collective-permute-start | bytes 393224 | tf_op jit(solution)/shard_map/ppermute | solution.py:455
  73.1 2.1 %collective-permute-start.4 = (bf16[256,256]{1,0:T(8,128)(2,1)}, bf16[256,256]{1,0:T(8,128)(2,1)S(1)}, u32[]{:S(2)}, u32[]{:S(2)}) collective-permute-start(bf16[256,256]{1,0:T(8,128)(2,1)} %get-tuple-element.27), channel_id=1, source_target_pairs={{0,64},{16,80},{32,96},{48,112},{64,0},{80,16},{96,32},{112,48},{1... | collective-permute-start | bytes 393224 | tf_op jit(solution)/shard_map/ppermute | solution.py:451
  75.2 1.6 %collective-permute-start.5 = (bf16[256,256]{1,0:T(8,128)(2,1)}, bf16[256,256]{1,0:T(8,128)(2,1)S(1)}, u32[]{:S(2)}, u32[]{:S(2)}) collective-permute-start(bf16[256,256]{1,0:T(8,128)(2,1)} %get-tuple-element.28), channel_id=1, source_target_pairs={{0,32},{16,48},{32,64},{48,80},{64,96},{80,112},{96,0},{112,16},{1... | collective-permute-start | bytes 393224 | tf_op jit(solution)/shard_map/ppermute | solution.py:451
  76.8 1.7 %collective-permute-start.6 = (bf16[256,256]{1,0:T(8,128)(2,1)}, bf16[256,256]{1,0:T(8,128)(2,1)S(1)}, u32[]{:S(2)}, u32[]{:S(2)}) collective-permute-start(bf16[256,256]{1,0:T(8,128)(2,1)} %get-tuple-element.29), channel_id=1, source_target_pairs={{0,96},{16,112},{32,0},{48,16},{64,32},{80,48},{96,64},{112,80},{1... | collective-permute-start | bytes 393224 | tf_op jit(solution)/shard_map/ppermute | solution.py:451
  78.5 4.6 %all-to-all-done.1.back_ref = bf16[16,2,128,256]{3,2,1,0:T(8,128)(2,1)S(1)} async-done(((bf16[16,2,128,256]{3,2,1,0:T(8,128)(2,1)}), bf16[16,2,128,256]{3,2,1,0:T(8,128)(2,1)S(1)}, u32[]{:S(2)}, u32[]{:S(2)}) %all-to-all-start.1) | async-done | bytes 2097184 | tf_op jit(solution)/shard_map/all_to_all | solution.py:465
  83.1 1.2 %copy-done.2 = bf16[1,128,4096]{2,1,0:T(8,128)(2,1)S(1)} copy-done((bf16[1,128,4096]{2,1,0:T(8,128)(2,1)S(1)}, bf16[1,128,4096]{2,1,0:T(8,128)(2,1)}, u32[]{:S(2)}) %copy-start.2) | copy-done | bytes 1048600
  84.3 1.5 %outputs.1 = (bf16[1,128,4096]{2,1,0:T(8,128)(2,1)}, bf16[1,128,4096]{2,1,0:T(8,128)(2,1)}) custom-call(bf16[16,2,128,256]{3,2,1,0:T(8,128)(2,1)S(1)} %all-to-all-done.1.back_ref, bf16[1,128,4096]{2,1,0:T(8,128)(2,1)S(1)} %copy-done.2), custom_call_target="tpu_custom_call" | custom-call | tf_op jit(solution)/shard_map/outputs/pallas_call | solution.py:431
  85.8 0.8 convert_add_fusion
  (11 shorter events, 0.0 us)
Async XLA Ops:
  3.5 6.6 %copy-start = (bf16[16,256,256]{2,1,0:T(8,128)(2,1)S(1)}, bf16[16,256,256]{2,1,0:T(8,128)(2,1)}, u32[]{:S(2)}) copy-start(bf16[16,256,256]{2,1,0:T(8,128)(2,1)} %constant.2.clone.forward_ref.forward_hbm) | copy-start | bytes 6291460
  3.5 35.4 %all-to-all-start = ((bf16[16,2,128,256]{3,2,1,0:T(8,128)(2,1)}), bf16[16,2,128,256]{3,2,1,0:T(8,128)(2,1)}, u32[]{:S(2)}, u32[]{:S(2)}) async-start(bf16[16,2,128,256]{3,2,1,0:T(8,128)(2,1)} %product.1), calls=%async_computation | async-start | bytes 4194304 | tf_op jit(solution)/shard_map/all_to_all | solution.py:462
  10.2 1.6 %copy-start.3 = (f32[2048,256]{1,0:T(8,128)S(1)}, f32[2048,256]{1,0:T(8,128)}, u32[]{:S(2)}) copy-start(f32[2048,256]{1,0:T(8,128)} %taps_ref.1) | copy-start | bytes 6291460
  13.8 1.4 %copy-start.1 = (bf16[16,256,256]{2,1,0:T(8,128)(2,1)}, bf16[16,256,256]{2,1,0:T(8,128)(2,1)S(1)}, u32[]{:S(2)}) copy-start(bf16[16,256,256]{2,1,0:T(8,128)(2,1)S(1)} %taps_spectrum.1.taps_hbm) | copy-start | bytes 6291460
  48.3 34.8 %all-to-all-start.1 = ((bf16[16,2,128,256]{3,2,1,0:T(8,128)(2,1)}), bf16[16,2,128,256]{3,2,1,0:T(8,128)(2,1)S(1)}, u32[]{:S(2)}, u32[]{:S(2)}) async-start(bf16[16,2,128,256]{3,2,1,0:T(8,128)(2,1)} %get-tuple-element.17), calls=%async_computation.1 | async-start | bytes 4194304 | tf_op jit(solution)/shard_map/all_to_all | solution.py:465
  58.6 27.3 %copy-start.4 = (bf16[256,256]{1,0:T(8,128)(2,1)S(1)}, bf16[256,256]{1,0:T(8,128)(2,1)}, u32[]{:S(2)}) copy-start(bf16[256,256]{1,0:T(8,128)(2,1)} %get-tuple-element.26) | copy-start | bytes 393220
  58.6 8.1 %collective-permute-start = (bf16[256,256]{1,0:T(8,128)(2,1)}, bf16[256,256]{1,0:T(8,128)(2,1)S(1)}, u32[]{:S(2)}, u32[]{:S(2)}) collective-permute-start(bf16[256,256]{1,0:T(8,128)(2,1)} %get-tuple-element.21), channel_id=1, source_target_pairs={{0,64},{16,80},{32,96},{48,112},{64,0},{80,16},{96,32},{112,48},{1... | collective-permute-start | bytes 393224 | tf_op jit(solution)/shard_map/ppermute | solution.py:451
  61.8 7.3 %collective-permute-start.1 = (bf16[256,256]{1,0:T(8,128)(2,1)}, bf16[256,256]{1,0:T(8,128)(2,1)S(1)}, u32[]{:S(2)}, u32[]{:S(2)}) collective-permute-start(bf16[256,256]{1,0:T(8,128)(2,1)} %get-tuple-element.22), channel_id=1, source_target_pairs={{0,32},{16,48},{32,64},{48,80},{64,96},{80,112},{96,0},{112,16},{1... | collective-permute-start | bytes 393224 | tf_op jit(solution)/shard_map/ppermute | solution.py:451
  62.5 6.8 %collective-permute-start.2 = (bf16[256,256]{1,0:T(8,128)(2,1)}, bf16[256,256]{1,0:T(8,128)(2,1)S(1)}, u32[]{:S(2)}, u32[]{:S(2)}) collective-permute-start(bf16[256,256]{1,0:T(8,128)(2,1)} %get-tuple-element.23), channel_id=1, source_target_pairs={{0,96},{16,112},{32,0},{48,16},{64,32},{80,48},{96,64},{112,80},{1... | collective-permute-start | bytes 393224 | tf_op jit(solution)/shard_map/ppermute | solution.py:451
  70.3 15.5 %collective-permute-start.3 = (bf16[256,256]{1,0:T(8,128)(2,1)S(1)}, bf16[256,256]{1,0:T(8,128)(2,1)S(1)}, u32[]{:S(2)}, u32[]{:S(2)}) collective-permute-start(bf16[256,256]{1,0:T(8,128)(2,1)S(1)} %add_convert_fusion), channel_id=1, source_target_pairs={{0,16},{16,0},{32,48},{48,32},{64,80},{80,64},{96,112},{112,96},{1... | collective-permute-start | bytes 393224 | tf_op jit(solution)/shard_map/ppermute | solution.py:455
  73.1 12.7 %collective-permute-start.4 = (bf16[256,256]{1,0:T(8,128)(2,1)}, bf16[256,256]{1,0:T(8,128)(2,1)S(1)}, u32[]{:S(2)}, u32[]{:S(2)}) collective-permute-start(bf16[256,256]{1,0:T(8,128)(2,1)} %get-tuple-element.27), channel_id=1, source_target_pairs={{0,64},{16,80},{32,96},{48,112},{64,0},{80,16},{96,32},{112,48},{1... | collective-permute-start | bytes 393224 | tf_op jit(solution)/shard_map/ppermute | solution.py:451
  75.2 10.6 %collective-permute-start.5 = (bf16[256,256]{1,0:T(8,128)(2,1)}, bf16[256,256]{1,0:T(8,128)(2,1)S(1)}, u32[]{:S(2)}, u32[]{:S(2)}) collective-permute-start(bf16[256,256]{1,0:T(8,128)(2,1)} %get-tuple-element.28), channel_id=1, source_target_pairs={{0,32},{16,48},{32,64},{48,80},{64,96},{80,112},{96,0},{112,16},{1... | collective-permute-start | bytes 393224 | tf_op jit(solution)/shard_map/ppermute | solution.py:451
  76.8 9.0 %collective-permute-start.6 = (bf16[256,256]{1,0:T(8,128)(2,1)}, bf16[256,256]{1,0:T(8,128)(2,1)S(1)}, u32[]{:S(2)}, u32[]{:S(2)}) collective-permute-start(bf16[256,256]{1,0:T(8,128)(2,1)} %get-tuple-element.29), channel_id=1, source_target_pairs={{0,96},{16,112},{32,0},{48,16},{64,32},{80,48},{96,64},{112,80},{1... | collective-permute-start | bytes 393224 | tf_op jit(solution)/shard_map/ppermute | solution.py:451
  83.1 1.2 %copy-start.2 = (bf16[1,128,4096]{2,1,0:T(8,128)(2,1)S(1)}, bf16[1,128,4096]{2,1,0:T(8,128)(2,1)}, u32[]{:S(2)}) copy-start(bf16[1,128,4096]{2,1,0:T(8,128)(2,1)} %cotangent_ref.3) | copy-start | bytes 3145732
